TPU v7x, 32 devices: a whole 2x2x4 slice. The times are simulated.
32 devices in a mesh: grp: 4 (over y, x), dev: 8 (over z, core).
Axes of the slice: x: 2, y: 2, z: 4, core: 2. Of those that a mesh axis runs over, the one named last changes fastest.
Arguments:
- canvas: bfloat16 [256, 1024, 256], P('grp', 'dev'), may hold values from -6 to 6
- conv_weight: bfloat16 [2304, 256], replicated, may hold values from -0.125 to 0.125
- conv_bias: float32 [256], replicated, may hold values from -3 to 3
- score_weight: float32 [256], replicated, may hold values from -0.75 to 0.75
- tile_tokens: bfloat16 [1024, 24, 3200], P(('grp', 'dev')), may hold values from -6 to 6
- tile_cell: int32 [4, 256], P('grp', 'dev'), may hold values from 0 to 8191
- tile_count: int32 [4, 8], P('grp'), may hold values from 1 to 32, 64 in all within a row
- holder_order: int32 [4, 8], P('grp'), may hold values from 0 to 7, each once within a row
- tile_image: int32 [4, 64], P('grp'), may hold values from 0 to 31, never falling along the last dimension, each value on 1 to 9 neighbouring positions
- ln_gain: float32 [3200], replicated, may hold values from 0.25 to 1.75
- qkv_weight: bfloat16 [3200, 4992], P(('grp', 'dev')), may hold values from -2 to 2
Outputs:
- score_map: float32 [256, 1024], P('grp', 'dev')
- attended: bfloat16 [6144, 1664], P(('grp', 'dev'))
Inputs may be any that keep to these rules, and one draw needn't show every extreme that they name: `tile_count`: the counts of one group add up to 64; in each group one device holds exactly 32. `tile_image`: ids never fall along a group's held tiles; each image has 1 to 9 tiles and one has exactly 9.
All inputs are finite; a program needn't handle non-finite values.
Results may differ from a plain program's by a relative error of at most 0.012.
Values may be sent and summed in bfloat16 or wider, within the bound.
A program may use at most 192 MiB of HBM per device.

v0:
```python
import math

import jax
import jax.numpy as jnp
from jax import lax
from jax.sharding import PartitionSpec as P

HD = 128
HEADS = 13
MT = 8


def with_halo(value, sides, width):
    for axis, dim in sides:
        size, length = (lax.axis_size(axis), value.shape[dim])
        up = [(i, (i + 1) % size) for i in range(size - 1)]
        down = [(j, i) for i, j in up]
        last = lax.slice_in_dim(value, length - width, length, axis=dim)
        initial = lax.slice_in_dim(value, 0, width, axis=dim)
        before = lax.ppermute(last, axis, up)
        after = lax.ppermute(initial, axis, down)
        value = jnp.concatenate([before, value, after], axis=dim)
    return value


def layer_norm(rows, gain):
    values = rows.astype(jnp.float32)
    center = jnp.mean(values, axis=1, keepdims=True)
    spread = jnp.mean(jnp.square(values - center), axis=1, keepdims=True)
    return ((values - center) * lax.rsqrt(spread + 1e-06) * gain).astype(jnp.bfloat16)


def conv_scores(padded, conv_weight, conv_bias, score_weight, height, breadth):
    channels = padded.shape[2]
    summed = jnp.zeros((height * breadth, conv_weight.shape[1]), jnp.float32)
    for row_off in range(3):
        for col_off in range(3):
            window = padded[row_off : row_off + height, col_off : col_off + breadth].reshape(
                height * breadth, channels
            )
            offset = (row_off * 3 + col_off) * channels
            summed = summed + jnp.dot(
                window, conv_weight[offset : offset + channels], preferred_element_type=jnp.float32
            )
    hidden = jax.nn.gelu(summed + conv_bias)
    return jnp.dot(hidden, score_weight, precision=lax.Precision.HIGHEST)


def attend(queries, keys, values, query_ids, key_ids):
    rows = queries.shape[0]
    query_heads = queries.reshape(rows, HEADS, HD)
    key_heads = keys.reshape(keys.shape[0], HEADS, HD)
    value_heads = values.reshape(values.shape[0], HEADS, HD)
    logits = jnp.einsum(
        "qhd,khd->hqk", query_heads, key_heads, preferred_element_type=jnp.float32
    ) * (1.0 / math.sqrt(HD))
    same = query_ids[:, None] == key_ids[None, :]
    logits = jnp.where(same[None], logits, -1e30)
    peak = jnp.max(logits, axis=2, keepdims=True)
    weights = jnp.exp(logits - peak)
    probs = (weights / jnp.sum(weights, axis=2, keepdims=True)).astype(jnp.bfloat16)
    result = jnp.einsum("hqk,khd->qhd", probs, value_heads, preferred_element_type=jnp.float32)
    return result.astype(jnp.bfloat16).reshape(rows, HEADS * HD)


def key_scale(sharp, col_count, head_width):
    columns = jnp.arange(col_count, dtype=jnp.int32)
    is_key = (columns >= head_width) & (columns < 2 * head_width)
    return jnp.where(is_key[None, :], sharp[:, None], 1.0)


def shards(
    canvas,
    conv_weight,
    conv_bias,
    score_weight,
    tile_tokens,
    tile_cell,
    tile_count,
    holder_order,
    tile_image,
    ln_gain,
    qkv_weight,
):
    height, breadth = (canvas.shape[0], canvas.shape[1])
    padded = with_halo(canvas, (("grp", 0), ("dev", 1)), 1)
    score_flat = conv_scores(padded, conv_weight, conv_bias, score_weight, height, breadth)
    score_map = score_flat.reshape(height, breadth)
    holders = lax.axis_size("dev")
    own_index = lax.axis_index("dev")
    slot_count = tile_tokens.shape[0]
    tile_len = tile_tokens.shape[1]
    model_width = tile_tokens.shape[2]
    per_peer = max(1, slot_count // holders)
    counts = tile_count[0]
    order = holder_order[0]
    prefix = jnp.cumsum(counts) - counts
    slot_range = jnp.arange(slot_count, dtype=jnp.int32)
    round_range = jnp.arange(per_peer, dtype=jnp.int32)
    holder_range = jnp.arange(holders, dtype=jnp.int32)
    position = jnp.take(prefix, own_index) + slot_range
    is_live = slot_range < jnp.take(counts, own_index)
    target = jnp.take(order, position % holders)
    same_holder = target[None, None, :] == holder_range[:, None, None]
    same_round = (slot_range // holders)[None, None, :] == round_range[None, :, None]
    send_mask = (same_holder & same_round & is_live[None, None, :]).astype(jnp.bfloat16)
    send_tiles = jnp.einsum(
        "kcs,std->kctd", send_mask, tile_tokens, preferred_element_type=jnp.float32
    ).astype(jnp.bfloat16)
    tile_score = jnp.take(score_flat, tile_cell[0]).astype(jnp.bfloat16)
    send_score = jnp.einsum(
        "kcs,s->kc", send_mask, tile_score, preferred_element_type=jnp.float32
    ).astype(jnp.bfloat16)
    recv_tiles, recv_score = (
        lax.all_to_all(send_tiles, "dev", split_axis=0, concat_axis=0, tiled=True),
        lax.all_to_all(send_score, "dev", split_axis=0, concat_axis=0, tiled=True),
    )
    place = jnp.sum(jnp.where(order == own_index, holder_range, 0))
    wanted = jnp.arange(MT, dtype=jnp.int32) * holders + place
    from_source = (prefix[None, :] <= wanted[:, None]) & (
        wanted[:, None] < (prefix + counts)[None, :]
    )
    round_of = (wanted[:, None] - prefix[None, :]) // holders
    take_mask = (
        from_source[:, :, None] & (round_of[:, :, None] == round_range[None, None, :])
    ).astype(jnp.bfloat16)
    held = jnp.einsum(
        "mjc,jctd->mtd", take_mask, recv_tiles, preferred_element_type=jnp.float32
    ).astype(jnp.bfloat16)
    held_rows = MT * tile_len
    held = held.reshape(held_rows, model_width)
    held_score = jnp.einsum(
        "mjc,jc->m", take_mask, recv_score, preferred_element_type=jnp.float32
    ).astype(jnp.bfloat16)
    sharpness = jnp.repeat(0.5 + jax.nn.softplus(held_score.astype(jnp.float32)), tile_len)
    normed = layer_norm(held, ln_gain)
    width_all = qkv_weight.shape[1]
    head_width = width_all // 3
    mixed = jnp.dot(
        normed,
        lax.all_gather(qkv_weight, ("grp", "dev"), axis=0, tiled=True),
        preferred_element_type=jnp.float32,
    )
    projected = (mixed * key_scale(sharpness, width_all, head_width)).astype(jnp.bfloat16)
    queries = projected[:, :head_width]
    near = with_halo(projected[:, head_width:], (("dev", 0),), held_rows)
    all_ids = tile_image[0]
    tile_total = all_ids.shape[0]
    near_tiles = own_index * MT - MT + jnp.arange(3 * MT, dtype=jnp.int32)
    inside = (near_tiles >= 0) & (near_tiles < tile_total)
    near_ids = jnp.where(inside, jnp.take(all_ids, jnp.clip(near_tiles, 0, tile_total - 1)), -1)
    key_ids = jnp.repeat(near_ids, tile_len)
    own_ids = jnp.repeat(
        jnp.take(all_ids, own_index * MT + jnp.arange(MT, dtype=jnp.int32)), tile_len
    )
    attended = attend(queries, near[:, :head_width], near[:, head_width:], own_ids, key_ids)
    return (score_map, attended)


def solution(mesh):
    placed = (
        P("grp", "dev", None),
        P(),
        P(),
        P(),
        P(("grp", "dev"), None, None),
        P("grp", "dev"),
        P("grp", None),
        P("grp", None),
        P("grp", None),
        P(),
        P(("grp", "dev"), None),
    )
    return jax.shard_map(
        shards,
        mesh=mesh,
        in_specs=placed,
        out_specs=(P("grp", "dev"), P(("grp", "dev"), None)),
        check_vma=False,
    )
```

profile of v0, /device:TPU:1, one launch (start us, length us, event | category | flops | bytes accessed | tf_op | source)
XLA Modules:
  0.0 413.1 jit_solution(13809198275469693596)
XLA Ops:
  7.2 0.7 all-gather.3.cloned.1.call-update
  7.9 0.9 fusion.94
  8.8 3.9 collective-permute-start
  12.8 1.3 collective-permute-start.1
  14.1 1.2 constant_dynamic-slice_fusion
  15.3 0.8 reduce-window.4
  19.3 1.4 gather_fusion
  20.7 6.4 %pad_maximum_fusion.3 = (bf16[64,128,256]{2,1,0:T(8,128)(2,1)S(1)}, bf16[64,128,256]{2,1,0:T(8,128)(2,1)S(1)}, bf16[66,128,256]{2,1,0:T(8,128)(2,1)S(1)}) fusion(bf16[64,128,256]{2,1,0:T(8,128)(2,1)} %param.11, bf16[1,128,256]{2,1,0:T(8,128)(2,1)S(1)} %collective-permute-done, bf16[1,128,256]{2,1,0:T(8,128)(2,1)S(1)} %collective-permute-done.1, ...), kind=kLoop, calls=%fused_computation.45 | loop fusion | flops 16777216 | bytes 16908288 | tf_op jit(solution)/shard_map/concatenate | solution.py:22
  27.3 3.9 collective-permute-start.2
  31.2 1.9 collective-permute-start.3
  33.1 2.2 fusion.44
  35.3 2.2 fusion.37
  37.5 2.6 collective-permute-done.3
  40.0 13.0 %pad_maximum_fusion.2 = (bf16[64,128,256]{2,1,0:T(8,128)(2,1)}, bf16[64,128,256]{2,1,0:T(8,128)(2,1)}, bf16[64,128,256]{2,1,0:T(8,128)(2,1)}, bf16[64,128,256]{2...) fusion(bf16[66,128,256]{2,1,0:T(8,128)(2,1)S(1)} %constant_dynamic-update-slice_fusion, ...), kind=kLoop, calls=%fused_computation.44 | loop fusion | flops 50331648 | bytes 29558784 | tf_op jit(solution)/shard_map/concatenate | solution.py:22
  53.0 4.6 %fusion.35 = f32[8192,256]{1,0:T(8,128)} fusion(bf16[8192,256]{1,0:T(8,128)(2,1)S(1)} %bitcast.130, bf16[2304,256]{1,0:T(8,128)(2,1)S(1)} %copy-done.8), kind=kOutput, calls=%fused_computation.67 | convolution fusion | flops 1073741824 | bytes 12713984 | tf_op jit(solution)/shard_map/dot_general | solution.py:42
  57.6 1.3 convolution_add_fusion.5
  58.9 3.7 convolution_add_fusion.4
  62.6 3.7 convolution_add_fusion.3
  66.3 1.3 convolution_add_fusion.2
  67.6 3.6 convolution_add_fusion.1
  71.2 9.1 %fusion.10 = f32[8192,256]{1,0:T(8,128)} fusion(f32[8192,256]{1,0:T(8,128)} %fusion.35, f32[8192,256]{1,0:T(8,128)S(1)} %fusion.37, f32[8192,256]{1,0:T(8,128)S(1)} %convolution_add_fusion.1, bf16[8192,256]{1,0:T(8,128)(2,1)} %bitcast.131, f32[256]{0:T(256)S(1)} %copy-done.10, bf16[2304,256]{1,0:T(8,128)(2,1)} %param.12), kind=kOutput, calls=%fused_computation.21 | convolution fusion | flops 1098907648 | bytes 37880832 | tf_op jit(solution)/shard_map/dot_general | solution.py:42
  80.4 10.4 %fusion.98 = f32[1,8192]{1,0:T(1,128)S(1)} fusion(f32[8192,256]{1,0:T(8,128)} %fusion.10, f32[256,1]{0,1:T(1,128)S(1)} %bitcast.119), kind=kOutput, calls=%fused_computation.179 | convolution fusion | flops 25165824 | bytes 8422400 | tf_op jit(solution)/shard_map/dot_general | solution.py:46
  90.8 0.7 gather_fusion.1
  91.7 0.7 copy.45
  92.4 3.3 all-to-all-start.1
  95.7 3.8 convolution_convert_fusion
  99.5 4.1 copy.39
  103.6 5.5 %all-to-all-start = ((bf16[8,4,24,3200]{3,1,2,0:T(4,128)(2,1)}), bf16[8,4,24,3200]{3,1,2,0:T(4,128)(2,1)}, u32[]{:S(2)}, u32[]{:S(2)}) async-start(bf16[8,4,24,3200]{3,1,2,0:T(4,128)(2,1)} %copy.39), calls=%async_computation | async-start | bytes 9830400 | tf_op jit(solution)/shard_map/all_to_all | solution.py:115
  110.9 195.2 %all-to-all-done = bf16[8,4,24,3200]{3,1,2,0:T(4,128)(2,1)} async-done(((bf16[8,4,24,3200]{3,1,2,0:T(4,128)(2,1)}), bf16[8,4,24,3200]{3,1,2,0:T(4,128)(2,1)}, u32[]{:S(2)}, u32[]{:S(2)}) %all-to-all-start) | async-done | bytes 4915232 | tf_op jit(solution)/shard_map/all_to_all | solution.py:115
  306.1 5.4 %fusion.96 = (f32[8,24]{0,1:T(8,128)S(1)}, f32[8,24,3200]{2,0,1:T(8,128)S(1)}) fusion(bf16[8,4,24,3200]{3,1,2,0:T(4,128)(2,1)} %all-to-all-done, s32[8,8]{1,0:T(8,128)S(1)} %add_select_fusion, pred[8,8]{1,0:T(8,128)(4,1)S(1)} %compare_and_fusion), kind=kOutput, calls=%fused_computation.177 | convolution fusion | flops 41165120 | bytes 7373888 | tf_op jit(solution)/shard_map/mjc,jctd->mtd/dot_general | solution.py:127
  311.8 1.9 copy.41
  314.2 2.1 fusion.27
  316.4 28.4 %reshape.563 = bf16[3200,4992]{1,0:T(8,128)(2,1)} reshape(bf16[32,100,4992]{2,1,0:T(8,128)(2,1)} %all-gather.3.cloned.1.call-done) | data formatting | bytes 63897600
  344.8 13.7 %fusion.11 = bf16[192,4992]{1,0:T(8,128)(2,1)S(1)} fusion(bf16[192,3200]{1,0:T(8,128)(2,1)S(1)} %fusion.27, bf16[3200,4992]{1,0:T(8,128)(2,1)} %reshape.563, f32[192]{0:T(256)S(1)} %broadcast_in_dim.102, pred[4992]{0:T(1024)(128)(4,1)S(1)} %fusion.47), kind=kOutput, calls=%fused_computation.31 | convolution fusion | flops 6137044992 | bytes 35100288 | tf_op jit(solution)/shard_map/dot_general | solution.py:139
  358.5 1.2 copy-done.7
  359.7 1.9 collective-permute-start.4
  361.6 2.5 collective-permute-start.5
  364.2 0.7 gather_fusion.3
  366.0 9.8 %collective-permute-done.4 = bf16[192,3328]{1,0:T(8,128)(2,1)S(1)} collective-permute-done((bf16[192,3328]{1,0:T(8,128)(2,1)S(1)}, bf16[192,3328]{1,0:T(8,128)(2,1)S(1)}, u32[]{:S(2)}, u32[]{:S(2)}) %collective-permute-start.4) | collective-permute-done | bytes 1277984 | tf_op jit(solution)/shard_map/ppermute | solution.py:20
  375.8 4.5 %collective-permute-done.5 = bf16[192,3328]{1,0:T(8,128)(2,1)} collective-permute-done((bf16[192,3328]{1,0:T(8,128)(2,1)S(1)}, bf16[192,3328]{1,0:T(8,128)(2,1)}, u32[]{:S(2)}, u32[]{:S(2)}) %collective-permute-start.5) | collective-permute-done | bytes 1277984 | tf_op jit(solution)/shard_map/ppermute | solution.py:21
  380.3 1.7 pad_maximum_fusion.4
  382.0 2.2 fusion.95
  384.2 3.4 copy.48
  387.5 4.8 %fusion.32 = f32[13,192,576]{2,1,0:T(8,128)} fusion(bf16[576,13,128]{0,2,1:T(8,128)(2,1)S(1)} %bitcast.134, bf16[192,4992]{1,0:T(8,128)(2,1)} %copy-done.7), kind=kOutput, calls=%fused_computation.62 | convolution fusion | flops 368050176 | bytes 8306688 | tf_op jit(solution)/shard_map/qhd,khd->hqk/dot_general | solution.py:54
  392.3 3.4 copy.47
  395.7 8.0 %fusion.97 = (f32[13,192]{1,0:T(8,128)S(1)}, f32[13,192,576]{2,1,0:T(8,128)S(1)}) fusion(f32[13,192,576]{2,1,0:T(8,128)} %fusion.32, pred[192,576]{1,0:T(8,128)(4,1)S(1)} %broadcast_compare_fusion), kind=kOutput, calls=%fused_computation.178 | output fusion | flops 8626751 | bytes 11622144 | tf_op jit(solution)/shard_map/sub | solution.py:60
  403.7 1.3 fusion.29
  405.0 0.9 copy.78
  (76 shorter events, 6.2 us)
Async XLA Ops:
  7.2 73.2 %copy-start = (f32[256]{0:T(256)S(1)}, f32[256]{0:T(256)}, u32[]{:S(2)}) copy-start(f32[256]{0:T(256)} %param.14) | copy-start | bytes 3076
  7.2 309.2 %all-gather.3.cloned.1.call-start = ((), (), s32[]{:S(2)}) async-start(), calls=%async_computation.2 | async-start | bytes 34265088 | tf_op jit(solution)/shard_map/all_gather | solution.py:141
  8.8 11.9 %collective-permute-start = (bf16[1,128,256]{2,1,0:T(8,128)(2,1)S(1)}, bf16[1,128,256]{2,1,0:T(8,128)(2,1)S(1)}, u32[]{:S(2)}, u32[]{:S(2)}) collective-permute-start(bf16[1,128,256]{2,1,0:T(8,128)(2,1)S(1)} %get-tuple-element.39), channel_id=1, source_target_pairs={{0,8},{8,16},{16,24},{1,9},{9,17},{17,25},{2,10},{10,18},{18,26},{... | collective-permute-start | bytes 196616 | tf_op jit(solution)/shard_map/ppermute | solution.py:20
  12.8 8.0 %collective-permute-start.1 = (bf16[1,128,256]{2,1,0:T(8,128)(2,1)S(1)}, bf16[1,128,256]{2,1,0:T(8,128)(2,1)S(1)}, u32[]{:S(2)}, u32[]{:S(2)}) collective-permute-start(bf16[1,128,256]{2,1,0:T(8,128)(2,1)S(1)} %get-tuple-element.38), channel_id=1, source_target_pairs={{8,0},{16,8},{24,16},{9,1},{17,9},{25,17},{10,2},{18,10},{26,18},{... | collective-permute-start | bytes 196616 | tf_op jit(solution)/shard_map/ppermute | solution.py:21
  27.3 10.2 %collective-permute-start.2 = (bf16[66,1,256]{2,1,0:T(2,128)(2,1)S(1)}, bf16[66,1,256]{2,1,0:T(2,128)(2,1)S(1)}, u32[]{:S(2)}, u32[]{:S(2)}) collective-permute-start(bf16[66,1,256]{2,1,0:T(2,128)(2,1)S(1)} %get-tuple-element.33), channel_id=1, source_target_pairs={{0,1},{1,2},{2,3},{3,4},{4,5},{5,6},{6,7},{8,9},{9,10},{10,11},{11... | collective-permute-start | bytes 101384 | tf_op jit(solution)/shard_map/ppermute | solution.py:20
  31.2 8.8 %collective-permute-start.3 = (bf16[66,1,256]{2,1,0:T(2,128)(2,1)S(1)}, bf16[66,1,256]{2,1,0:T(2,128)(2,1)S(1)}, u32[]{:S(2)}, u32[]{:S(2)}) collective-permute-start(bf16[66,1,256]{2,1,0:T(2,128)(2,1)S(1)} %get-tuple-element.34), channel_id=1, source_target_pairs={{1,0},{2,1},{3,2},{4,3},{5,4},{6,5},{7,6},{9,8},{10,9},{11,10},{12... | collective-permute-start | bytes 101384 | tf_op jit(solution)/shard_map/ppermute | solution.py:21
  37.5 15.5 %copy-start.8 = (bf16[2304,256]{1,0:T(8,128)(2,1)S(1)}, bf16[2304,256]{1,0:T(8,128)(2,1)}, u32[]{:S(2)}) copy-start(bf16[2304,256]{1,0:T(8,128)(2,1)} %param.12) | copy-start | bytes 3538948
  53.0 4.6 %copy-start.5 = (bf16[64,128,256]{2,1,0:T(8,128)(2,1)S(1)}, bf16[64,128,256]{2,1,0:T(8,128)(2,1)}, u32[]{:S(2)}) copy-start(bf16[64,128,256]{2,1,0:T(8,128)(2,1)} %get-tuple-element.25) | copy-start | bytes 12582916
  62.5 3.8 copy-start.4
  67.6 3.6 copy-start.10
  80.4 11.2 %copy-start.11 = (s32[1,32]{1,0:T(1,128)S(1)}, s32[1,32]{1,0:T(1,128)}, u32[]{:S(2)}) copy-start(s32[1,32]{1,0:T(1,128)} %param.16) | copy-start | bytes 388
  90.8 8.7 %copy-start.6 = (f32[1,8192]{1,0:T(1,128)}, f32[1,8192]{1,0:T(1,128)S(1)}, u32[]{:S(2)}) copy-start(f32[1,8192]{1,0:T(1,128)S(1)} %fusion.98) | copy-start | bytes 98308
  92.4 11.2 %all-to-all-start.1 = ((bf16[8,1,4]{2,1,0:T(2,128)(2,1)}), bf16[8,1,4]{2,1,0:T(2,128)(2,1)S(1)}, u32[]{:S(2)}, u32[]{:S(2)}) async-start(bf16[8,1,4]{2,1,0:T(2,128)(2,1)} %copy.45), calls=%async_computation.1 | async-start | bytes 8192 | tf_op jit(solution)/shard_map/all_to_all | solution.py:116
  103.6 5.5 %copy-start.3 = (s32[1,8]{1,0:T(1,128)S(1)}, s32[1,8]{1,0:T(1,128)}, u32[]{:S(2)}) copy-start(s32[1,8]{1,0:T(1,128)} %param.18) | copy-start | bytes 100
  103.6 6.8 %copy-start.12 = (s32[1,8]{1,0:T(1,128)S(1)}, s32[1,8]{1,0:T(1,128)}, u32[]{:S(2)}) copy-start(s32[1,8]{1,0:T(1,128)} %param.17) | copy-start | bytes 100
  103.6 202.6 %all-to-all-start = ((bf16[8,4,24,3200]{3,1,2,0:T(4,128)(2,1)}), bf16[8,4,24,3200]{3,1,2,0:T(4,128)(2,1)}, u32[]{:S(2)}, u32[]{:S(2)}) async-start(bf16[8,4,24,3200]{3,1,2,0:T(4,128)(2,1)} %copy.39), calls=%async_computation | async-start | bytes 9830400 | tf_op jit(solution)/shard_map/all_to_all | solution.py:115
  311.5 2.7 copy-start.9
  344.7 19.4 %copy-start.2 = (s32[1,64]{1,0:T(1,128)S(1)}, s32[1,64]{1,0:T(1,128)}, u32[]{:S(2)}) copy-start(s32[1,64]{1,0:T(1,128)} %param.19) | copy-start | bytes 772
  358.4 1.3 copy-start.7
  359.7 16.1 %collective-permute-start.4 = (bf16[192,3328]{1,0:T(8,128)(2,1)S(1)}, bf16[192,3328]{1,0:T(8,128)(2,1)S(1)}, u32[]{:S(2)}, u32[]{:S(2)}) collective-permute-start(bf16[192,3328]{1,0:T(8,128)(2,1)S(1)} %slice.136), channel_id=1, source_target_pairs={{0,1},{1,2},{2,3},{3,4},{4,5},{5,6},{6,7},{8,9},{9,10},{10,11},{11... | collective-permute-start | bytes 3833864 | tf_op jit(solution)/shard_map/ppermute | solution.py:20
  361.6 18.7 %collective-permute-start.5 = (bf16[192,3328]{1,0:T(8,128)(2,1)S(1)}, bf16[192,3328]{1,0:T(8,128)(2,1)}, u32[]{:S(2)}, u32[]{:S(2)}) collective-permute-start(bf16[192,3328]{1,0:T(8,128)(2,1)S(1)} %slice.136), channel_id=1, source_target_pairs={{1,0},{2,1},{3,2},{4,3},{5,4},{6,5},{7,6},{9,8},{10,9},{11,10},{12... | collective-permute-start | bytes 3833864 | tf_op jit(solution)/shard_map/ppermute | solution.py:21
  403.7 2.2 copy-start.1
Sparse Core Ops, SparseCore 0:
  10.9 290.3 all-gather.2
where the time goes:
time: 417 us; the launch traced here: 413 us
  waiting for transfers between devices  213 us (51%)
  matrix products  71.2 us (17%)
  local copies, waits for them, and re-layouts  53.4 us (13%)
  other arithmetic  35.4 us (8%)
  starting transfers between devices  24.2 us (6%)
  between operations  16 us (4%)
    all_to_all x1, waiting for transfers between devices, shards(): lax.all_to_all(send_tiles, 'dev', split_axis=0, concat_axis=0, tiled=True)  195 us
    dot_general x9, matrix products, conv_scores(): jnp.dot(window, conv_weight[offset:offset + channels], preferred_element_...  31.6 us
    unnamed x28, local copies, waits for them, and re-layouts  29.6 us
    concatenate x3, other arithmetic, with_halo(): value = jnp.concatenate([before, value, after], axis=dim)  21 us
    dot_general x1, matrix products, shards(): jnp.dot(normed, lax.all_gather(qkv_weight, ('grp', 'dev'), axis=0, tiled=...  13.7 us
    dot_general x1, matrix products, conv_scores(): return jnp.dot(hidden, score_weight, precision=lax.Precision.HIGHEST)  10.4 us
    ppermute x3, waiting for transfers between devices, with_halo(): before = lax.ppermute(last, axis, up)  9.79 us
    ppermute x3, starting transfers between devices, with_halo(): before = lax.ppermute(last, axis, up)  9.76 us
  transfers between devices with their start and end apart: 9, of which 4 were waited for; matrix products, arithmetic and copies ran while one was open for 22% of the time, Pallas kernels for 0%

commit v1 on v0

v1 whole, which is shorter than its diff:
```python
import math

import jax
import jax.numpy as jnp
from jax import lax
from jax.sharding import Mesh
from jax.sharding import PartitionSpec as P

HD = 128
HEADS = 13
MT = 8
PART = (HEADS + 1) // 2
ROW_PAD = 16


def line_exchange(last, initial, axis):
    size = lax.axis_size(axis)
    up = [(i, i + 1) for i in range(size - 1)]
    down = [(j, i) for i, j in up]
    return lax.ppermute(last, axis, up), lax.ppermute(initial, axis, down)


def dev_exchange(last, initial, axes):
    size = lax.axis_size(axes)
    up = [(i, i + 1) for i in range(size - 1)]
    down = [(j, i) for i, j in up]
    return lax.ppermute(last, axes, up), lax.ppermute(initial, axes, down)


def with_halo(value, axes, dim):
    length = value.shape[dim]
    before, after = dev_exchange(
        lax.slice_in_dim(value, length - 1, length, axis=dim),
        lax.slice_in_dim(value, 0, 1, axis=dim),
        axes,
    )
    return jnp.concatenate([before, value, after], axis=dim)


def swap_core(value):
    return lax.ppermute(value, "core", [(0, 1), (1, 0)])


def layer_norm(rows, gain):
    values = rows.astype(jnp.float32)
    center = jnp.mean(values, axis=1, keepdims=True)
    spread = jnp.mean(jnp.square(values - center), axis=1, keepdims=True)
    return ((values - center) * lax.rsqrt(spread + 1e-06) * gain).astype(jnp.bfloat16)


def conv_scores(padded, conv_weight, conv_bias, score_weight, height, breadth):
    channels = padded.shape[2]
    summed = jnp.zeros((height * breadth, conv_weight.shape[1]), jnp.float32)
    for row_off in range(3):
        for col_off in range(3):
            window = padded[row_off : row_off + height, col_off : col_off + breadth].reshape(
                height * breadth, channels
            )
            offset = (row_off * 3 + col_off) * channels
            summed = summed + jnp.dot(
                window, conv_weight[offset : offset + channels], preferred_element_type=jnp.float32
            )
    hidden = jax.nn.gelu(summed + conv_bias)
    return jnp.dot(hidden, score_weight, precision=lax.Precision.HIGHEST)


def attend(queries, keys, values, query_ids, key_ids):
    logits = jnp.einsum("bqhd,bkhd->bhqk", queries, keys, preferred_element_type=jnp.float32) * (
        1.0 / math.sqrt(HD)
    )
    same = query_ids[:, :, None] == key_ids[:, None, :]
    logits = jnp.where(same[:, None], logits, -1e30)
    peak = jnp.max(logits, axis=3, keepdims=True)
    weights = jnp.exp(logits - peak)
    probs = (weights / jnp.sum(weights, axis=3, keepdims=True)).astype(jnp.bfloat16)
    result = jnp.einsum("bhqk,bkhd->bqhd", probs, values, preferred_element_type=jnp.float32)
    return result.astype(jnp.bfloat16)


def core_heads(weight, core):
    rows = weight.shape[0]
    split = weight.reshape(rows, 3, HEADS, HD)
    low = split[:, :, :PART].reshape(rows, 3 * PART * HD)
    high = split[:, :, HEADS - PART :].reshape(rows, 3 * PART * HD)
    mine = jnp.where(core == 0, low, high)
    other = jnp.where(core == 0, high, low)
    return mine, other


def shards(
    canvas,
    conv_weight,
    conv_bias,
    score_weight,
    tile_tokens,
    tile_cell,
    tile_count,
    holder_order,
    tile_image,
    ln_gain,
    qkv_weight,
):
    dev = ("chip", "core")
    core = lax.axis_index("core")
    chip = lax.axis_index("chip")
    holders = lax.axis_size(dev)
    own_index = chip * 2 + core
    slot_count, tile_len, model_width = tile_tokens.shape
    rows_here = qkv_weight.shape[0]

    mine, other = core_heads(qkv_weight, core)
    theirs = swap_core(other)
    first = jnp.where(core == 0, mine, theirs)
    second = jnp.where(core == 0, theirs, mine)
    chip_rows = 2 * rows_here
    padded_rows = -(-chip_rows // ROW_PAD) * ROW_PAD
    fill = jnp.zeros((padded_rows - chip_rows, first.shape[1]), first.dtype)
    block = jnp.concatenate([first, second, fill], axis=0)
    weights = lax.all_gather(block, ("grp", "chip"), axis=0, tiled=True)

    per_peer = max(1, slot_count // holders)
    counts = tile_count[0]
    order = holder_order[0]
    slot_range = jnp.arange(slot_count, dtype=jnp.int32)
    round_range = jnp.arange(per_peer, dtype=jnp.int32)
    holder_range = jnp.arange(holders, dtype=jnp.int32)
    prefix = jnp.sum(
        jnp.where(holder_range[None, :] < holder_range[:, None], counts[None, :], 0), axis=1
    )
    is_me = holder_range == own_index
    position = jnp.sum(jnp.where(is_me, prefix, 0)) + slot_range
    is_live = slot_range < jnp.sum(jnp.where(is_me, counts, 0))
    hit = (position % holders)[:, None] == holder_range[None, :]
    target = jnp.sum(jnp.where(hit, order[None, :], 0), axis=1)
    same_holder = target[None, None, :] == holder_range[:, None, None]
    same_round = (slot_range // holders)[None, None, :] == round_range[None, :, None]
    send_mask = (same_holder & same_round & is_live[None, None, :]).astype(jnp.bfloat16)
    send_tiles = jnp.einsum(
        "kcs,std->kctd", send_mask, tile_tokens, preferred_element_type=jnp.float32
    ).astype(jnp.bfloat16)
    send_tiles, canvas = lax.optimization_barrier((send_tiles, canvas))
    recv_tiles = lax.all_to_all(send_tiles, dev, split_axis=0, concat_axis=0, tiled=True)

    height, breadth = canvas.shape[0], canvas.shape[1]
    padded = with_halo(with_halo(canvas, "grp", 0), dev, 1)
    score_flat = conv_scores(padded, conv_weight, conv_bias, score_weight, height, breadth)
    score_map = score_flat.reshape(height, breadth)
    tile_score = jnp.take(score_flat, tile_cell[0]).astype(jnp.bfloat16)
    send_score = jnp.einsum(
        "kcs,s->kc", send_mask, tile_score, preferred_element_type=jnp.float32
    ).astype(jnp.bfloat16)
    recv_score = lax.all_to_all(send_score, dev, split_axis=0, concat_axis=0, tiled=True)

    place = jnp.sum(jnp.where(order == own_index, holder_range, 0))
    wanted = jnp.arange(MT, dtype=jnp.int32) * holders + place
    from_source = (prefix[None, :] <= wanted[:, None]) & (
        wanted[:, None] < (prefix + counts)[None, :]
    )
    round_of = (wanted[:, None] - prefix[None, :]) // holders
    take_mask = (
        from_source[:, :, None] & (round_of[:, :, None] == round_range[None, None, :])
    ).astype(jnp.bfloat16)
    held_score = jnp.einsum(
        "mjc,jc->m", take_mask, recv_score, preferred_element_type=jnp.float32
    ).astype(jnp.bfloat16)
    held = jnp.einsum(
        "mjc,jctd->mtd", take_mask, recv_tiles, preferred_element_type=jnp.float32
    ).astype(jnp.bfloat16)
    held_rows = MT * tile_len
    normed = layer_norm(held.reshape(held_rows, model_width), ln_gain)

    def both(value):
        far = swap_core(value)
        return jnp.concatenate(
            [jnp.where(core == 0, value, far), jnp.where(core == 0, far, value)], axis=0
        )

    chip_score = both(held_score)
    sharpness = jnp.repeat(0.5 + jax.nn.softplus(chip_score.astype(jnp.float32)), tile_len)
    chip_normed = both(normed)
    blocks = model_width // chip_rows
    chip_normed = jnp.pad(
        chip_normed.reshape(2 * held_rows, blocks, chip_rows),
        ((0, 0), (0, 0), (0, padded_rows - chip_rows)),
    ).reshape(2 * held_rows, blocks * padded_rows)

    mixed = jnp.dot(chip_normed, weights, preferred_element_type=jnp.float32)
    part = PART * HD
    queries = mixed[:, :part].astype(jnp.bfloat16)
    keys = (mixed[:, part : 2 * part] * sharpness[:, None]).astype(jnp.bfloat16)
    values = mixed[:, 2 * part :].astype(jnp.bfloat16)
    key_value = jnp.concatenate([keys, values], axis=1)
    before, after = line_exchange(key_value[held_rows:], key_value[:held_rows], "chip")
    near = jnp.concatenate([before, key_value, after], axis=0)
    near = jnp.stack([near[: 3 * held_rows], near[held_rows:]], axis=0)
    near = near.reshape(2, 3 * held_rows, 2, PART, HD)

    all_ids = tile_image[0]
    tile_total = all_ids.shape[0]
    chip_tiles = 2 * MT
    ids_pad = jnp.pad(all_ids, (MT, MT), constant_values=-1)
    near_ids = lax.dynamic_slice_in_dim(ids_pad, chip * chip_tiles, chip_tiles + 2 * MT)
    key_ids = jnp.stack([near_ids[: 3 * MT], near_ids[MT:]], axis=0)
    key_ids = jnp.repeat(key_ids, tile_len, axis=1)
    own_ids = jnp.repeat(near_ids[MT:-MT].reshape(2, MT), tile_len, axis=1)
    result = attend(
        queries.reshape(2, held_rows, PART, HD), near[:, :, 0], near[:, :, 1], own_ids, key_ids
    ).reshape(2, held_rows, part)
    mine_out = jnp.where(core == 0, result[0], result[1])
    far_out = swap_core(jnp.where(core == 0, result[1], result[0]))
    low = jnp.where(core == 0, mine_out, far_out)
    high = jnp.where(core == 0, far_out, mine_out)
    skip = (2 * PART - HEADS) * HD
    attended = jnp.concatenate([low, high[:, skip:]], axis=1)
    return (score_map, attended)


def solution(mesh):
    groups, devs = mesh.devices.shape
    fine = Mesh(mesh.devices.reshape(groups, devs // 2, 2), ("grp", "chip", "core"))
    dev = ("chip", "core")
    every = ("grp", "chip", "core")
    placed = (
        P("grp", dev, None),
        P(),
        P(),
        P(),
        P(every, None, None),
        P("grp", dev),
        P("grp", None),
        P("grp", None),
        P("grp", None),
        P(),
        P(every, None),
    )
    return jax.shard_map(
        shards,
        mesh=fine,
        in_specs=placed,
        out_specs=(P("grp", dev), P(every, None)),
        check_vma=False,
    )
```

time: 417 us -> 385 us (0.923)
  the two profiles are of different devices: /device:TPU:1 before, /device:TPU:0 now
where the time goes in v1:
time: 385 us; the launch traced here: 378 us
  waiting for transfers between devices  149 us (39%)
  matrix products  68.5 us (18%)
  blocking collectives  53.8 us (14%)
  other arithmetic  41.9 us (11%)
  local copies, waits for them, and re-layouts  29.7 us (8%)
  starting transfers between devices  19.7 us (5%)
  between operations  15 us (4%)
    all_to_all x1, waiting for transfers between devices, shards(): lax.all_to_all(send_tiles, dev, split_axis=0, concat_axis=0, tiled=True)  129 us
    all_to_all x1, blocking collectives, shards(): lax.all_to_all(send_score, dev, split_axis=0, concat_axis=0, tiled=True)  53.8 us
    dot_general x9, matrix products, conv_scores(): jnp.dot(window, conv_weight[offset:offset + channels], preferred_element_...  31.7 us
    concatenate x2, other arithmetic, with_halo(): return jnp.concatenate([before, value, after], axis=dim)  18.6 us
    ppermute x2, waiting for transfers between devices, line_exchange(): return (lax.ppermute(last, axis, up), lax.ppermute(initial, axis, down))  16.5 us
    dot_general x1, matrix products, shards(): mixed = jnp.dot(chip_normed, weights, preferred_element_type=jnp.float32)  11.3 us
    dot_general x1, matrix products, conv_scores(): return jnp.dot(hidden, score_weight, precision=lax.Precision.HIGHEST)  10.4 us
    ppermute x4, starting transfers between devices, dev_exchange(): return (lax.ppermute(last, axes, up), lax.ppermute(initial, axes, down))  9.76 us
  transfers between devices with their start and end apart: 12, of which 7 were waited for; matrix products, arithmetic and copies ran while one was open for 25% of the time, Pallas kernels for 0%

profile of v1, /device:TPU:0, one launch (start us, length us, event | category | flops | bytes accessed | tf_op | source)
XLA Modules:
  0.0 378.0 jit_solution(16731685832040127071)
XLA Ops:
  7.2 2.4 reshape.345
  11.7 0.9 collective-permute-done.5
  12.7 1.3 maximum_maximum_fusion.1
  16.3 3.8 %convolution_convert_fusion = bf16[8,4,24,3200]{3,0,2,1:T(8,128)(2,1)S(1)} fusion(bf16[32,24,3200]{2,1,0:T(8,128)(2,1)} %param.15, pred[32]{0:T(512)(128)(4,1)S(1)} %iota_compare_fusion.5, pred[4,32]{1,0:T(4,128)(4,1)S(1)} %iota_compare_fusion.4, pred[8,32]{1,0:T(8,128)(4,1)S(1)} %iota_compare_fusion.1), kind=kOutput, calls=%fused_computation.22 | convolution fusion | flops 159746048 | bytes 9830816 | tf_op jit(solution)/shard_map/kcs,std->kctd/dot_general | solution.py:138
  20.1 0.9 fusion.87
  21.0 4.8 %collective-permute-start = (bf16[1,128,256]{2,1,0:T(8,128)(2,1)S(1)}, bf16[1,128,256]{2,1,0:T(8,128)(2,1)S(1)}, u32[]{:S(2)}, u32[]{:S(2)}) collective-permute-start(bf16[1,128,256]{2,1,0:T(8,128)(2,1)S(1)} %get-tuple-element.23), channel_id=1, source_target_pairs={{0,8},{8,16},{16,24},{1,9},{9,17},{17,25},{2,10},{10,18},{18,26},{... | collective-permute-start | bytes 196616 | tf_op jit(solution)/shard_map/ppermute | solution.py:27
  25.8 1.3 collective-permute-start.1
  27.1 2.7 copy.57
  29.8 5.0 %all-to-all-start = ((bf16[8,4,24,3200]{3,2,1,0:T(8,128)(2,1)}), bf16[8,4,24,3200]{3,2,1,0:T(8,128)(2,1)}, u32[]{:S(2)}, u32[]{:S(2)}) async-start(bf16[8,4,24,3200]{3,2,1,0:T(8,128)(2,1)} %copy.57), calls=%async_computation | async-start | bytes 9830400 | tf_op jit(solution)/shard_map/all_to_all | solution.py:142
  36.4 5.9 %pad_maximum_fusion.3 = (bf16[64,128,256]{2,1,0:T(8,128)(2,1)S(1)}, bf16[64,128,256]{2,1,0:T(8,128)(2,1)S(1)}, bf16[66,128,256]{2,1,0:T(8,128)(2,1)S(1)}) fusion(bf16[64,128,256]{2,1,0:T(8,128)(2,1)} %param.11, bf16[1,128,256]{2,1,0:T(8,128)(2,1)S(1)} %collective-permute-done, bf16[1,128,256]{2,1,0:T(8,128)(2,1)S(1)} %collective-permute-done.1, ...), kind=kLoop, calls=%fused_computation.41 | loop fusion | flops 16777216 | bytes 16908288 | tf_op jit(solution)/shard_map/concatenate | solution.py:37
  42.4 2.4 collective-permute-start.2
  44.8 1.3 collective-permute-start.3
  46.1 2.2 fusion.44
  48.3 2.2 fusion.37
  50.5 12.7 %pad_maximum_fusion.2 = (bf16[64,128,256]{2,1,0:T(8,128)(2,1)}, bf16[64,128,256]{2,1,0:T(8,128)(2,1)}, bf16[64,128,256]{2,1,0:T(8,128)(2,1)}, bf16[64,128,256]{2...) fusion(bf16[66,128,256]{2,1,0:T(8,128)(2,1)S(1)} %constant_dynamic-update-slice_fusion, ...), kind=kLoop, calls=%fused_computation.40 | loop fusion | flops 50331648 | bytes 29558784 | tf_op jit(solution)/shard_map/concatenate | solution.py:37
  63.2 4.6 %fusion.35 = f32[8192,256]{1,0:T(8,128)} fusion(bf16[8192,256]{1,0:T(8,128)(2,1)S(1)} %bitcast.126, bf16[2304,256]{1,0:T(8,128)(2,1)S(1)} %copy-done.6), kind=kOutput, calls=%fused_computation.85 | convolution fusion | flops 1073741824 | bytes 12713984 | tf_op jit(solution)/shard_map/dot_general | solution.py:60
  67.8 1.3 convolution_add_fusion.5
  69.1 3.7 convolution_add_fusion.4
  72.7 3.7 convolution_add_fusion.3
  76.5 1.3 convolution_add_fusion.2
  77.8 3.6 convolution_add_fusion.1
  81.4 9.2 %fusion.10 = f32[8192,256]{1,0:T(8,128)} fusion(f32[8192,256]{1,0:T(8,128)} %fusion.35, f32[8192,256]{1,0:T(8,128)S(1)} %fusion.37, f32[8192,256]{1,0:T(8,128)S(1)} %convolution_add_fusion.1, bf16[8192,256]{1,0:T(8,128)(2,1)} %bitcast.127, f32[256]{0:T(256)S(1)} %copy-done.8, bf16[2304,256]{1,0:T(8,128)(2,1)} %param.12), kind=kOutput, calls=%fused_computation.18 | convolution fusion | flops 1098907648 | bytes 37880832 | tf_op jit(solution)/shard_map/dot_general | solution.py:60
  90.6 129.0 %all-to-all-done = bf16[8,4,24,3200]{3,2,1,0:T(8,128)(2,1)} async-done(((bf16[8,4,24,3200]{3,2,1,0:T(8,128)(2,1)}), bf16[8,4,24,3200]{3,2,1,0:T(8,128)(2,1)}, u32[]{:S(2)}, u32[]{:S(2)}) %all-to-all-start) | async-done | bytes 4915232 | tf_op jit(solution)/shard_map/all_to_all | solution.py:142
  219.6 6.8 %fusion.89 = (f32[8,24]{0,1:T(8,128)S(1)}, f32[8,24,3200]{2,0,1:T(8,128)}) fusion(bf16[8,4,24,3200]{3,2,1,0:T(8,128)(2,1)} %all-to-all-done, s32[8,8]{1,0:T(8,128)S(1)} %add_select_fusion, pred[8,8]{1,0:T(8,128)(4,1)S(1)} %compare_and_fusion), kind=kOutput, calls=%fused_computation.185 | convolution fusion | flops 41165120 | bytes 7373888 | tf_op jit(solution)/shard_map/mjc,jctd->mtd/dot_general | solution.py:166
  226.7 2.3 copy.59
  229.7 1.5 fusion.27
  231.2 10.4 %fusion.92 = f32[1,8192]{1,0:T(1,128)S(1)} fusion(f32[8192,256]{1,0:T(8,128)} %fusion.10, f32[256,1]{0,1:T(1,128)S(1)} %bitcast.118), kind=kOutput, calls=%fused_computation.188 | convolution fusion | flops 25165824 | bytes 8422400 | tf_op jit(solution)/shard_map/dot_general | solution.py:64
  242.6 53.8 %all_to_all.17 = bf16[8,1,4]{2,1,0:T(2,128)(2,1)S(1)} all-to-all(bf16[8,1,4]{2,1,0:T(2,128)(2,1)S(1)} %copy.64), channel_id=1, replica_groups=mesh['grp'=4,'chip'=4,'core'=2] {'chip','core'}, dimensions={0} | all-to-all | bytes 128 | tf_op jit(solution)/shard_map/all_to_all | solution.py:152
  296.6 1.1 collective-permute-done.6
  298.0 2.1 broadcast_select_fusion.1
  300.3 2.8 copy.63
  303.1 1.9 pad.8
  305.3 11.3 %fusion.90 = (bf16[384,2688]{1,0:T(8,128)(2,1)S(1)}, f32[384,2688]{1,0:T(8,128)S(1)}) fusion(bf16[384,3328]{0,1:T(8,128)(2,1)S(1)} %bitcast.128, bf16[3328,2688]{1,0:T(8,128)(2,1)} %all-gather.2.cloned.1.call-done), kind=kOutput, calls=%fused_computation.186 | convolution fusion | flops 6871302144 | bytes 26640384 | tf_op jit(solution)/shard_map/dot_general | solution.py:187
  316.9 1.2 pad_maximum_fusion.6
  318.1 3.1 collective-permute-start.7
  321.2 1.3 collective-permute-start.8
  324.1 11.6 %collective-permute-done.7 = bf16[192,1792]{1,0:T(8,128)(2,1)} collective-permute-done((bf16[192,1792]{1,0:T(8,128)(2,1)}, bf16[192,1792]{1,0:T(8,128)(2,1)}, u32[]{:S(2)}, u32[]{:S(2)}) %collective-permute-start.7) | collective-permute-done | bytes 688160 | tf_op jit(solution)/shard_map/ppermute | solution.py:20
  335.7 4.9 %collective-permute-done.8 = bf16[192,1792]{1,0:T(8,128)(2,1)} collective-permute-done((bf16[192,1792]{1,0:T(8,128)(2,1)}, bf16[192,1792]{1,0:T(8,128)(2,1)}, u32[]{:S(2)}, u32[]{:S(2)}) %collective-permute-start.8) | collective-permute-done | bytes 688160 | tf_op jit(solution)/shard_map/ppermute | solution.py:20
  340.6 7.5 %pad_maximum_fusion.5 = (bf16[576,1792]{1,0:T(8,128)(2,1)}, bf16[576,1792]{1,0:T(8,128)(2,1)}) fusion(bf16[192,1792]{1,0:T(8,128)(2,1)} %collective-permute-done.8, bf16[384,896]{1,0:T(8,128)(2,1)S(1)} %get-tuple-element.27, bf16[384,896]{1,0:T(8,128)(2,1)S(1)} %fusion.29, bf16[192,1792]{1,0:T(8,128)(2,1)} %collective-permute-done.7), kind=kLoop, calls=%fused_computation.56 | loop fusion | flops 12386304 | bytes 6881280 | tf_op jit(solution)/shard_map/concatenate | solution.py:194
  348.1 3.9 %stack.18 = bf16[1,576,2,7,128]{4,3,2,1,0:T(8,128)(2,1)S(1)} reshape(bf16[576,1792]{1,0:T(8,128)(2,1)} %get-tuple-element.29) | data formatting | bytes 4128768 | tf_op jit(solution)/shard_map/stack | solution.py:195
  352.0 1.9 copy_dynamic-update-slice_fusion.1
  353.9 3.9 %stack.19 = bf16[1,576,2,7,128]{4,3,2,1,0:T(8,128)(2,1)S(1)} reshape(bf16[576,1792]{1,0:T(8,128)(2,1)} %get-tuple-element.28) | data formatting | bytes 4128768 | tf_op jit(solution)/shard_map/stack | solution.py:195
  357.9 1.9 copy_dynamic-update-slice_fusion
  359.7 2.7 fusion.28
  362.5 3.7 fusion.91
  366.1 1.4 fusion.31
  368.3 1.4 collective-permute-done.9
  369.8 0.9 pad_maximum_fusion.7
  (100 shorter events, 11.5 us)
Async XLA Ops:
  7.2 224.0 %copy-start = (f32[256]{0:T(256)S(1)}, f32[256]{0:T(256)}, u32[]{:S(2)}) copy-start(f32[256]{0:T(256)} %param.14) | copy-start | bytes 3076
  7.2 298.1 %all-gather.2.cloned.1.call-start = ((), (), s32[]{:S(2)}) async-start(), calls=%async_computation.2 | async-start | bytes 19009536 | tf_op jit(solution)/shard_map/all_gather | solution.py:119
  9.8 4.3 %copy-start.9 = (s32[1,8]{1,0:T(1,128)S(1)}, s32[1,8]{1,0:T(1,128)}, u32[]{:S(2)}) copy-start(s32[1,8]{1,0:T(1,128)} %param.17) | copy-start | bytes 100
  9.9 6.3 %copy-start.10 = (s32[1,8]{1,0:T(1,128)S(1)}, s32[1,8]{1,0:T(1,128)}, u32[]{:S(2)}) copy-start(s32[1,8]{1,0:T(1,128)} %param.18) | copy-start | bytes 100
  10.5 2.1 collective-permute-start.5
  21.0 15.3 %collective-permute-start = (bf16[1,128,256]{2,1,0:T(8,128)(2,1)S(1)}, bf16[1,128,256]{2,1,0:T(8,128)(2,1)S(1)}, u32[]{:S(2)}, u32[]{:S(2)}) collective-permute-start(bf16[1,128,256]{2,1,0:T(8,128)(2,1)S(1)} %get-tuple-element.23), channel_id=1, source_target_pairs={{0,8},{8,16},{16,24},{1,9},{9,17},{17,25},{2,10},{10,18},{18,26},{... | collective-permute-start | bytes 196616 | tf_op jit(solution)/shard_map/ppermute | solution.py:27
  25.8 10.6 %collective-permute-start.1 = (bf16[1,128,256]{2,1,0:T(8,128)(2,1)S(1)}, bf16[1,128,256]{2,1,0:T(8,128)(2,1)S(1)}, u32[]{:S(2)}, u32[]{:S(2)}) collective-permute-start(bf16[1,128,256]{2,1,0:T(8,128)(2,1)S(1)} %get-tuple-element.22), channel_id=1, source_target_pairs={{8,0},{16,8},{24,16},{9,1},{17,9},{25,17},{10,2},{18,10},{26,18},{... | collective-permute-start | bytes 196616 | tf_op jit(solution)/shard_map/ppermute | solution.py:27
  29.8 6.3 %copy-start.11 = (s32[1,32]{1,0:T(1,128)S(1)}, s32[1,32]{1,0:T(1,128)}, u32[]{:S(2)}) copy-start(s32[1,32]{1,0:T(1,128)} %param.16) | copy-start | bytes 388
  29.8 189.8 %all-to-all-start = ((bf16[8,4,24,3200]{3,2,1,0:T(8,128)(2,1)}), bf16[8,4,24,3200]{3,2,1,0:T(8,128)(2,1)}, u32[]{:S(2)}, u32[]{:S(2)}) async-start(bf16[8,4,24,3200]{3,2,1,0:T(8,128)(2,1)} %copy.57), calls=%async_computation | async-start | bytes 9830400 | tf_op jit(solution)/shard_map/all_to_all | solution.py:142
  42.4 8.1 %collective-permute-start.2 = (bf16[66,1,256]{2,1,0:T(2,128)(2,1)S(1)}, bf16[66,1,256]{2,1,0:T(2,128)(2,1)S(1)}, u32[]{:S(2)}, u32[]{:S(2)}) collective-permute-start(bf16[66,1,256]{2,1,0:T(2,128)(2,1)S(1)} %get-tuple-element.17), channel_id=1, source_target_pairs={{0,1},{1,2},{2,3},{3,4},{4,5},{5,6},{6,7},{8,9},{9,10},{10,11},{11... | collective-permute-start | bytes 101384 | tf_op jit(solution)/shard_map/ppermute | solution.py:27
  44.8 5.7 %collective-permute-start.3 = (bf16[66,1,256]{2,1,0:T(2,128)(2,1)S(1)}, bf16[66,1,256]{2,1,0:T(2,128)(2,1)S(1)}, u32[]{:S(2)}, u32[]{:S(2)}) collective-permute-start(bf16[66,1,256]{2,1,0:T(2,128)(2,1)S(1)} %get-tuple-element.18), channel_id=1, source_target_pairs={{1,0},{2,1},{3,2},{4,3},{5,4},{6,5},{7,6},{9,8},{10,9},{11,10},{12... | collective-permute-start | bytes 101384 | tf_op jit(solution)/shard_map/ppermute | solution.py:27
  50.5 12.7 %copy-start.6 = (bf16[2304,256]{1,0:T(8,128)(2,1)S(1)}, bf16[2304,256]{1,0:T(8,128)(2,1)}, u32[]{:S(2)}) copy-start(bf16[2304,256]{1,0:T(8,128)(2,1)} %param.12) | copy-start | bytes 3538948
  63.2 4.6 %copy-start.2 = (bf16[64,128,256]{2,1,0:T(8,128)(2,1)S(1)}, bf16[64,128,256]{2,1,0:T(8,128)(2,1)}, u32[]{:S(2)}) copy-start(bf16[64,128,256]{2,1,0:T(8,128)(2,1)} %get-tuple-element.9) | copy-start | bytes 12582916
  72.7 3.8 copy-start.1
  77.8 3.6 copy-start.8
  226.4 3.2 copy-start.7
  226.7 2.4 copy-start.3
  231.2 66.8 %collective-permute-start.4 = (bf16[192,3200]{1,0:T(8,128)(2,1)}, bf16[192,3200]{1,0:T(8,128)(2,1)}, u32[]{:S(2)}, u32[]{:S(2)}) collective-permute-start(bf16[192,3200]{1,0:T(8,128)(2,1)} %fusion.27), channel_id=1, source_target_pairs={{0,1},{1,0},{2,3},{3,2},{4,5},{5,4},{6,7},{7,6},{8,9},{9,8},{10,11... | collective-permute-start | bytes 3686408 | tf_op jit(solution)/shard_map/ppermute | solution.py:41
  241.6 58.7 %copy-start.4 = (f32[1,8192]{1,0:T(1,128)}, f32[1,8192]{1,0:T(1,128)S(1)}, u32[]{:S(2)}) copy-start(f32[1,8192]{1,0:T(1,128)S(1)} %fusion.92) | copy-start | bytes 98308
  296.6 1.1 collective-permute-start.6
  316.6 5.8 %copy-start.12 = (s32[1,64]{1,0:T(1,128)S(1)}, s32[1,64]{1,0:T(1,128)}, u32[]{:S(2)}) copy-start(s32[1,64]{1,0:T(1,128)} %param.19) | copy-start | bytes 772
  318.1 17.6 %collective-permute-start.7 = (bf16[192,1792]{1,0:T(8,128)(2,1)}, bf16[192,1792]{1,0:T(8,128)(2,1)}, u32[]{:S(2)}, u32[]{:S(2)}) collective-permute-start(bf16[192,1792]{1,0:T(8,128)(2,1)} %get-tuple-element.31), channel_id=1, source_target_pairs={{0,2},{2,4},{4,6},{1,3},{3,5},{5,7},{8,10},{10,12},{12,14},{9,11},... | collective-permute-start | bytes 2064392 | tf_op jit(solution)/shard_map/ppermute | solution.py:20
  321.2 19.5 %collective-permute-start.8 = (bf16[192,1792]{1,0:T(8,128)(2,1)}, bf16[192,1792]{1,0:T(8,128)(2,1)}, u32[]{:S(2)}, u32[]{:S(2)}) collective-permute-start(bf16[192,1792]{1,0:T(8,128)(2,1)} %get-tuple-element.30), channel_id=1, source_target_pairs={{2,0},{4,2},{6,4},{3,1},{5,3},{7,5},{10,8},{12,10},{14,12},{11,9},... | collective-permute-start | bytes 2064392 | tf_op jit(solution)/shard_map/ppermute | solution.py:20
  362.4 3.7 copy-start.5
  367.9 1.7 collective-permute-start.9
Sparse Core Ops, SparseCore 0:
  14.2 291.0 all-gather.1

commit v2 on v1

--- a/solution.py
+++ b/solution.py
@@ -87,7 +87,7 @@
     return mine, other
 
 
-def shards(
+def shards_by_core(
     canvas,
     conv_weight,
     conv_bias,
@@ -215,6 +215,172 @@
     return (score_map, attended)
 
 
+def prefix_of(counts, holder_range):
+    earlier = holder_range[None, :] < holder_range[:, None]
+    return jnp.sum(jnp.where(earlier, counts[None, :], 0), axis=1)
+
+
+def hop_pairs(hop, chips):
+    return [(hop, hop + 1), (chips - 1 - hop, chips - 2 - hop)]
+
+
+def merge_line(chunks, chips):
+    total = list(chunks)
+    got = [None] * len(chunks)
+    waves = []
+    for step in range(len(chunks) + chips - 2):
+        arrived = []
+        for hop in reversed(range(chips - 1)):
+            at = step - hop
+            if not 0 <= at < len(chunks):
+                continue
+            load = chunks[at] if hop == 0 else chunks[at] + got[at]
+            if len(waves) >= 2:
+                load, waves[-2] = lax.optimization_barrier((load, waves[-2]))
+            fresh = lax.ppermute(load, "chip", hop_pairs(hop, chips))
+            arrived.append((at, fresh))
+        for at, fresh in arrived:
+            got[at] = fresh
+            total[at] = total[at] + fresh
+        waves.append([fresh for _, fresh in arrived])
+    return total
+
+
+def shards_by_head(
+    canvas,
+    conv_weight,
+    conv_bias,
+    score_weight,
+    tile_tokens,
+    tile_cell,
+    tile_count,
+    holder_order,
+    tile_image,
+    ln_gain,
+    qkv_weight,
+):
+    dev = ("chip", "core")
+    core = lax.axis_index("core")
+    chips = lax.axis_size("chip")
+    holders = lax.axis_size(dev)
+    groups = lax.axis_size("grp")
+    group = lax.axis_index("grp")
+    own_index = lax.axis_index("chip") * 2 + core
+    slot_count, tile_len, model_width = tile_tokens.shape
+    rows_here = qkv_weight.shape[0]
+    each = -(-HEADS // holders)
+    wide = each * HD
+    first_head = [min(each * d, HEADS - each) for d in range(holders)]
+
+    counts = tile_count[0]
+    order = holder_order[0]
+    total = holders * MT
+    slot_range = jnp.arange(slot_count, dtype=jnp.int32)
+    holder_range = jnp.arange(holders, dtype=jnp.int32)
+    prefix = prefix_of(counts, holder_range)
+    is_me = holder_range == own_index
+    my_start = jnp.sum(jnp.where(is_me, prefix, 0))
+    my_count = jnp.sum(jnp.where(is_me, counts, 0))
+    place = jnp.sum(
+        jnp.where(order[None, :] == holder_range[:, None], holder_range[None, :], 0), axis=1
+    )
+    position = (
+        jnp.arange(MT, dtype=jnp.int32)[None, :] * holders + place[:, None]
+    ).reshape(total)
+    source_slot = position - my_start
+    source = (source_slot[:, None] == slot_range[None, :]) & (slot_range < my_count)[None, :]
+    source = source.astype(jnp.bfloat16)
+    half = total // 2
+    mine_mask = jnp.where(core == 0, source[:half], source[half:])
+    other_mask = jnp.where(core == 0, source[half:], source[:half])
+
+    def pick(mask):
+        return jnp.einsum(
+            "ps,std->ptd", mask, tile_tokens, preferred_element_type=jnp.float32
+        ).astype(jnp.bfloat16)
+
+    n_chunks = 8
+    per_chunk = half // n_chunks
+    given = pick(other_mask).reshape(half * tile_len, model_width)
+    kept = pick(mine_mask).reshape(half * tile_len, model_width)
+    chip_half = kept + swap_core(given)
+    chunk_rows = per_chunk * tile_len
+    chunks = [chip_half[i * chunk_rows : (i + 1) * chunk_rows] for i in range(n_chunks)]
+
+    split = qkv_weight.reshape(rows_here, 3, HEADS, HD)
+    send_weight = jnp.stack(
+        [split[:, :, h : h + each].reshape(rows_here, 3 * wide) for h in first_head], axis=0
+    )
+    chunks[0], send_weight = lax.optimization_barrier((chunks[0], send_weight))
+    block = lax.all_to_all(send_weight, dev, split_axis=0, concat_axis=0, tiled=True)
+    block = block.reshape(holders * rows_here, 3 * wide)
+    group_rows = holders * rows_here
+    weights = jnp.zeros((groups * group_rows, 3 * wide), jnp.bfloat16)
+    weights = lax.dynamic_update_slice_in_dim(weights, block, group * group_rows, 0)
+    for shift in range(1, groups):
+        far = lax.ppermute(block, "grp", [(i, (i + shift) % groups) for i in range(groups)])
+        weights = lax.dynamic_update_slice_in_dim(
+            weights, far, ((group - shift) % groups) * group_rows, 0
+        )
+
+    canvas, chunks[0] = lax.optimization_barrier((canvas, chunks[0]))
+    height, breadth = canvas.shape[0], canvas.shape[1]
+    padded = with_halo(with_halo(canvas, "grp", 0), dev, 1)
+    score_flat = conv_scores(padded, conv_weight, conv_bias, score_weight, height, breadth)
+    score_map = score_flat.reshape(height, breadth)
+    tile_score = jnp.take(score_flat, tile_cell[0]).astype(jnp.bfloat16)
+    own_scores = jnp.sum(source.astype(jnp.float32) * tile_score.astype(jnp.float32), axis=1)
+    held_score = lax.psum(own_scores, dev)
+    sharpness = jnp.repeat(0.5 + jax.nn.softplus(held_score), tile_len)
+
+    merged = merge_line(chunks, chips)
+    normed = [layer_norm(rows, ln_gain) for rows in merged]
+    far = [swap_core(rows) for rows in normed]
+    near_half, far_half = jnp.concatenate(normed, axis=0), jnp.concatenate(far, axis=0)
+    near_mixed = jnp.dot(near_half, weights, preferred_element_type=jnp.float32)
+    far_mixed = jnp.dot(far_half, weights, preferred_element_type=jnp.float32)
+    mixed = jnp.concatenate(
+        [jnp.where(core == 0, near_mixed, far_mixed), jnp.where(core == 0, far_mixed, near_mixed)],
+        axis=0,
+    )
+    queries = mixed[:, :wide].astype(jnp.bfloat16)
+    keys = (mixed[:, wide : 2 * wide] * sharpness[:, None]).astype(jnp.bfloat16)
+    values = mixed[:, 2 * wide :].astype(jnp.bfloat16)
+
+    held_rows = MT * tile_len
+    token_ids = jnp.repeat(tile_image[0], tile_len)
+
+    def banded(value, fill):
+        edge = [(held_rows, held_rows)] + [(0, 0)] * (value.ndim - 1)
+        blocks = jnp.pad(value, edge, constant_values=fill)
+        blocks = blocks.reshape((holders + 2, held_rows) + value.shape[1:])
+        return jnp.concatenate([blocks[:-2], blocks[1:-1], blocks[2:]], axis=1)
+
+    key_ids = banded(token_ids, -1)
+    own_ids = token_ids.reshape(holders, held_rows)
+    outs = []
+    for head in range(each):
+        lanes = slice(head * HD, (head + 1) * HD)
+        outs.append(
+            attend(
+                queries[:, lanes].reshape(holders, held_rows, 1, HD),
+                banded(keys[:, lanes], 0)[:, :, None],
+                banded(values[:, lanes], 0)[:, :, None],
+                own_ids,
+                key_ids,
+            )[:, :, 0]
+        )
+    mine = jnp.concatenate(outs, axis=2)
+    heads_in = lax.all_to_all(mine, dev, split_axis=0, concat_axis=0, tiled=True)
+    parts, done = [], 0
+    for d in range(holders):
+        if done < HEADS:
+            skip = done - first_head[d]
+            parts.append(heads_in[d][:, skip * HD :])
+            done = first_head[d] + each
+    return (score_map, jnp.concatenate(parts, axis=1))
+
+
 def solution(mesh):
     groups, devs = mesh.devices.shape
     fine = Mesh(mesh.devices.reshape(groups, devs // 2, 2), ("grp", "chip", "core"))
@@ -234,7 +400,7 @@
         P(every, None),
     )
     return jax.shard_map(
-        shards,
+        shards_by_head if devs <= HEADS else shards_by_core,
         mesh=fine,
         in_specs=placed,
         out_specs=(P("grp", dev), P(every, None)),

time: 385 us -> 502 us (1.30)
  starting transfers between devices: 19.7 us -> 121 us
  other arithmetic: 41.9 us -> 70.2 us
  between operations: 15 us -> 2.27 us
  blocking collectives: 53.8 us -> 61.9 us
  waiting for transfers between devices: 149 us -> 141 us
    all_to_all x1, waiting for transfers between devices: 129 us -> 0.01 us  [shards_by_head(): lax.all_to_all(send_weight, dev, split_axis=0, concat_axis=0, tiled=True)]
    ppermute x2 -> x27, waiting for transfers between devices: 16.5 us -> 128 us  [the longest x24 128 us: merge_line(): fresh = lax.ppermute(load, 'chip', hop_pairs(hop, chips))]
    ppermute x2 -> x27, starting transfers between devices: 4.33 us -> 103 us  [the longest x24 99.1 us: merge_line(): fresh = lax.ppermute(load, 'chip', hop_pairs(hop, chips))]
    psum x0 -> x1, blocking collectives: none -> 35.9 us  [shards_by_head(): held_score = lax.psum(own_scores, dev)]
    all_to_all x1, blocking collectives: 53.8 us -> 25.9 us  [shards_by_head(): lax.all_to_all(mine, dev, split_axis=0, concat_axis=0, tiled=True)]
    add x2 -> x7, other arithmetic: 0.74 us -> 18 us  [the longest x3 11.1 us: merge_line(): load = chunks[at] if hop == 0 else chunks[at] + got[at]]
    reduce_sum x4 -> x12, other arithmetic: 1.47 us -> 13.9 us  [the longest x8 10.9 us: layer_norm(): center = jnp.mean(values, axis=1, keepdims=True)]
    dot_general x6 -> x4, matrix products: 24.9 us -> 13.5 us  [the longest x2 5.29 us: pick(): jnp.einsum('ps,std->ptd', mask, tile_tokens, preferred_element_type=jnp.f...]
  transfers between devices with their start and end apart: 12 -> 41, of which waited for: 7 -> 16; matrix products, arithmetic and copies ran while one was open for 25% -> 23% of each run, Pallas kernels for 0% -> 0%
where the time goes in v2:
time: 502 us; the launch traced here: 492 us
  waiting for transfers between devices  141 us (28%)
  starting transfers between devices  121 us (24%)
  other arithmetic  70.2 us (14%)
  matrix products  68 us (14%)
  blocking collectives  61.9 us (12%)
  local copies, waits for them, and re-layouts  27.9 us (6%)
    ppermute x24, waiting for transfers between devices, merge_line(): fresh = lax.ppermute(load, 'chip', hop_pairs(hop, chips))  128 us
    ppermute x24, starting transfers between devices, merge_line(): fresh = lax.ppermute(load, 'chip', hop_pairs(hop, chips))  99.1 us
    psum x1, blocking collectives, shards_by_head(): held_score = lax.psum(own_scores, dev)  35.9 us
    dot_general x9, matrix products, conv_scores(): jnp.dot(window, conv_weight[offset:offset + channels], preferred_element_...  33.7 us
    concatenate x2, other arithmetic, with_halo(): return jnp.concatenate([before, value, after], axis=dim)  28.3 us
    all_to_all x1, blocking collectives, shards_by_head(): lax.all_to_all(mine, dev, split_axis=0, concat_axis=0, tiled=True)  25.9 us
    unnamed x86, local copies, waits for them, and re-layouts  12 us
    add x3, other arithmetic, merge_line(): load = chunks[at] if hop == 0 else chunks[at] + got[at]  11.1 us
  transfers between devices with their start and end apart: 41, of which 16 were waited for; matrix products, arithmetic and copies ran while one was open for 23% of the time, Pallas kernels for 0%

profile of v2, /device:TPU:0, one launch (start us, length us, event | category | flops | bytes accessed | tf_op | source)
XLA Modules:
  0.0 492.1 jit_solution(6131721177122409908)
XLA Ops:
  5.1 3.9 convolution_convert_fusion
  8.9 3.6 copy.22
  16.0 5.1 %collective-permute-done = bf16[768,3200]{1,0:T(8,128)(2,1)S(1)} collective-permute-done((bf16[768,3200]{1,0:T(8,128)(2,1)}, bf16[768,3200]{1,0:T(8,128)(2,1)S(1)}, u32[]{:S(2)}, u32[]{:S(2)}) %collective-permute-start) | collective-permute-done | bytes 4915232 | tf_op jit(solution)/shard_map/ppermute | solution.py:41
  22.2 2.2 copy-done.1
  24.5 5.7 %collective-permute-start.26 = (bf16[96,3200]{1,0:T(8,128)(2,1)S(1)}, bf16[96,3200]{1,0:T(8,128)(2,1)}, u32[]{:S(2)}, u32[]{:S(2)}) collective-permute-start(bf16[96,3200]{1,0:T(8,128)(2,1)S(1)} %slice.379), channel_id=1, source_target_pairs={{0,2},{6,4},{1,3},{7,5},{8,10},{14,12},{9,11},{15,13},{16,18},{22,... | collective-permute-start | bytes 1843208 | tf_op jit(solution)/shard_map/ppermute | solution.py:240
  31.9 10.8 %collective-permute-done.26 = bf16[96,3200]{1,0:T(8,128)(2,1)} collective-permute-done((bf16[96,3200]{1,0:T(8,128)(2,1)S(1)}, bf16[96,3200]{1,0:T(8,128)(2,1)}, u32[]{:S(2)}, u32[]{:S(2)}) %collective-permute-start.26) | collective-permute-done | bytes 614432 | tf_op jit(solution)/shard_map/ppermute | solution.py:240
  42.7 4.2 slice_add_fusion.1
  47.7 7.3 %collective-permute-start.11 = (bf16[96,3200]{1,0:T(8,128)(2,1)}, bf16[96,3200]{1,0:T(8,128)(2,1)S(1)}, u32[]{:S(2)}, u32[]{:S(2)}) collective-permute-start(bf16[96,3200]{1,0:T(8,128)(2,1)} %get-tuple-element.71), channel_id=1, source_target_pairs={{0,2},{6,4},{1,3},{7,5},{8,10},{14,12},{9,11},{15,13},{16,18},{22,... | collective-permute-start | bytes 1843208 | tf_op jit(solution)/shard_map/ppermute | solution.py:240
  60.5 2.1 collective-permute-start.14
  62.6 2.1 collective-permute-start.17
  64.7 2.1 collective-permute-start.20
  66.8 2.5 collective-permute-start.23
  69.6 5.1 %collective-permute-start.8 = (bf16[96,3200]{1,0:T(8,128)(2,1)}, bf16[96,3200]{1,0:T(8,128)(2,1)}, u32[]{:S(2)}, u32[]{:S(2)}) collective-permute-start(bf16[96,3200]{1,0:T(8,128)(2,1)} %get-tuple-element.72), channel_id=1, source_target_pairs={{0,2},{6,4},{1,3},{7,5},{8,10},{14,12},{9,11},{15,13},{16,18},{22,... | collective-permute-start | bytes 1843208 | tf_op jit(solution)/shard_map/ppermute | solution.py:240
  77.6 5.2 %collective-permute-done.14 = bf16[96,3200]{1,0:T(8,128)(2,1)} collective-permute-done((bf16[96,3200]{1,0:T(8,128)(2,1)}, bf16[96,3200]{1,0:T(8,128)(2,1)}, u32[]{:S(2)}, u32[]{:S(2)}) %collective-permute-start.14) | collective-permute-done | bytes 614432 | tf_op jit(solution)/shard_map/ppermute | solution.py:240
  82.8 13.2 %collective-permute-done.17 = bf16[96,3200]{1,0:T(8,128)(2,1)} collective-permute-done((bf16[96,3200]{1,0:T(8,128)(2,1)}, bf16[96,3200]{1,0:T(8,128)(2,1)}, u32[]{:S(2)}, u32[]{:S(2)}) %collective-permute-start.17) | collective-permute-done | bytes 614432 | tf_op jit(solution)/shard_map/ppermute | solution.py:240
  95.9 13.2 %collective-permute-done.20 = bf16[96,3200]{1,0:T(8,128)(2,1)} collective-permute-done((bf16[96,3200]{1,0:T(8,128)(2,1)}, bf16[96,3200]{1,0:T(8,128)(2,1)}, u32[]{:S(2)}, u32[]{:S(2)}) %collective-permute-start.20) | collective-permute-done | bytes 614432 | tf_op jit(solution)/shard_map/ppermute | solution.py:240
  109.1 13.2 %collective-permute-done.23 = bf16[96,3200]{1,0:T(8,128)(2,1)} collective-permute-done((bf16[96,3200]{1,0:T(8,128)(2,1)}, bf16[96,3200]{1,0:T(8,128)(2,1)}, u32[]{:S(2)}, u32[]{:S(2)}) %collective-permute-start.23) | collective-permute-done | bytes 614432 | tf_op jit(solution)/shard_map/ppermute | solution.py:240
  122.3 11.2 %collective-permute-done.8 = bf16[96,3200]{1,0:T(8,128)(2,1)} collective-permute-done((bf16[96,3200]{1,0:T(8,128)(2,1)}, bf16[96,3200]{1,0:T(8,128)(2,1)}, u32[]{:S(2)}, u32[]{:S(2)}) %collective-permute-start.8) | collective-permute-done | bytes 614432 | tf_op jit(solution)/shard_map/ppermute | solution.py:240
  133.4 5.6 %slice_add_fusion = (bf16[96,3200]{1,0:T(8,128)(2,1)}, bf16[96,3200]{1,0:T(8,128)(2,1)}, bf16[96,3200]{1,0:T(8,128)(2,1)}, bf16[96,3200]{1,0:T(8,128)(2,1)}, bf1...) fusion(bf16[96,3200]{1,0:T(8,128)(2,1)S(1)} %collective-permute-done., ...), kind=kLoop, calls=%fused_computation.282 | loop fusion | flops 2150400 | bytes 14131200 | tf_op jit(solution)/shard_map/add | solution.py:237
  139.9 3.4 collective-permute-start.1
  148.1 8.5 %all-to-all-start = ((bf16[8,100,768]{2,1,0:T(8,128)(2,1)}), bf16[8,100,768]{2,1,0:T(8,128)(2,1)}, u32[]{:S(2)}, u32[]{:S(2)}) async-start(bf16[8,100,768]{2,1,0:T(8,128)(2,1)} %constant_dynamic-update-slice_fusion), calls=%async_computation | async-start | bytes 2555904 | tf_op jit(solution)/shard_map/all_to_all | solution.py:315
  157.9 5.1 %collective-permute-done.2 = bf16[1,128,256]{2,1,0:T(8,128)(2,1)S(1)} collective-permute-done((bf16[1,128,256]{2,1,0:T(8,128)(2,1)S(1)}, bf16[1,128,256]{2,1,0:T(8,128)(2,1)S(1)}, u32[]{:S(2)}, u32[]{:S(2)}) %collective-permute-start.2) | collective-permute-done | bytes 65568 | tf_op jit(solution)/shard_map/ppermute | solution.py:27
  163.0 5.6 %pad_maximum_fusion.4 = (bf16[64,128,256]{2,1,0:T(8,128)(2,1)S(1)}, bf16[64,128,256]{2,1,0:T(8,128)(2,1)S(1)}, bf16[66,128,256]{2,1,0:T(8,128)(2,1)S(1)}) fusion(bf16[64,128,256]{2,1,0:T(8,128)(2,1)} %param.11, bf16[1,128,256]{2,1,0:T(8,128)(2,1)S(1)} %collective-permute-done.1, bf16[1,128,256]{2,1,0:T(8,128)(2,1)S(1)} %collective-permute-done.2, ...), kind=kLoop, calls=%fused_computation.42 | loop fusion | flops 16777216 | bytes 16908288 | tf_op jit(solution)/shard_map/concatenate | solution.py:37
  173.0 4.5 fusion.110
  179.0 39.6 %collective-permute-start.5 = (bf16[96,3200]{1,0:T(8,128)(2,1)}, bf16[96,3200]{1,0:T(8,128)(2,1)}, u32[]{:S(2)}, u32[]{:S(2)}) collective-permute-start(bf16[96,3200]{1,0:T(8,128)(2,1)} %get-tuple-element.16), channel_id=1, source_target_pairs={{0,2},{6,4},{1,3},{7,5},{8,10},{14,12},{9,11},{15,13},{16,18},{22,... | collective-permute-start | bytes 1843208 | tf_op jit(solution)/shard_map/ppermute | solution.py:240
  218.6 22.6 %pad_maximum_fusion.3 = (bf16[64,128,256]{2,1,0:T(8,128)(2,1)}, bf16[64,128,256]{2,1,0:T(8,128)(2,1)}, bf16[64,128,256]{2,1,0:T(8,128)(2,1)S(1)}, bf16[64,128,25...) fusion(bf16[66,128,256]{2,1,0:T(8,128)(2,1)} %copy-done.8, ...), kind=kLoop, calls=%fused_computation.41 | loop fusion | flops 50331648 | bytes 29558784 | tf_op jit(solution)/shard_map/concatenate | solution.py:37
  241.3 3.7 convolution_add_fusion.5
  244.9 3.7 convolution_add_fusion.4
  252.1 2.4 convolution_add_fusion.1
  254.5 5.5 %fusion.108 = f32[8192,256]{1,0:T(8,128)} fusion(bf16[8192,256]{1,0:T(8,128)(2,1)S(1)} %bitcast.116, bf16[2304,256]{1,0:T(8,128)(2,1)} %param.12), kind=kOutput, calls=%fused_computation.163 | convolution fusion | flops 1073741824 | bytes 12713984 | tf_op jit(solution)/shard_map/dot_general | solution.py:60
  261.6 12.6 %collective-permute-start.9 = (bf16[96,3200]{1,0:T(8,128)(2,1)}, bf16[96,3200]{1,0:T(8,128)(2,1)}, u32[]{:S(2)}, u32[]{:S(2)}) collective-permute-start(bf16[96,3200]{1,0:T(8,128)(2,1)} %get-tuple-element.59), channel_id=1, source_target_pairs={{2,4},{4,2},{3,5},{5,3},{10,12},{12,10},{11,13},{13,11},{18,20},{2... | collective-permute-start | bytes 1843208 | tf_op jit(solution)/shard_map/ppermute | solution.py:240
  274.3 9.9 %fusion.11 = f32[8192,256]{1,0:T(8,128)} fusion(f32[8192,256]{1,0:T(8,128)} %fusion.108, f32[8192,256]{1,0:T(8,128)} %fusion.110, f32[8192,256]{1,0:T(8,128)S(1)} %convolution_add_fusion.1, bf16[8192,256]{1,0:T(8,128)(2,1)S(1)} %bitcast.117, f32[256]{0:T(256)S(1)} %copy-done.23, bf16[2304,256]{1,0:T(8,128)(2,1)} %param.12), kind=kOutput, calls=%fused_computation.19 | convolution fusion | flops 1098907648 | bytes 37880832 | tf_op jit(solution)/shard_map/dot_general | solution.py:60
  286.5 4.3 slice_add_fusion.2
  294.7 7.1 %fusion.177 = f32[1,8192]{1,0:T(1,128)S(1)} fusion(f32[8192,256]{1,0:T(8,128)S(1)} %copy-done.2, f32[256,1]{0,1:T(1,128)S(1)} %bitcast.106), kind=kOutput, calls=%fused_computation.303 | convolution fusion | flops 25165824 | bytes 8422400 | tf_op jit(solution)/shard_map/dot_general | solution.py:64
  302.7 35.9 %psum.7 = f32[64]{0:T(128)S(1)} all-reduce(f32[64]{0:T(128)S(1)} %multiply_reduce_fusion), channel_id=1, replica_groups=mesh['grp'=4,'chip'=4,'core'=2] {'chip','core'}, use_global_device_ids=true, to_apply=%region_21.22 | all-reduce | flops 64 | bytes 512 | tf_op jit(solution)/shard_map/psum | solution.py:333
  350.5 7.3 %collective-permute-done.16 = bf16[96,3200]{1,0:T(8,128)(2,1)} collective-permute-done((bf16[96,3200]{1,0:T(8,128)(2,1)}, bf16[96,3200]{1,0:T(8,128)(2,1)}, u32[]{:S(2)}, u32[]{:S(2)}) %collective-permute-start.16) | collective-permute-done | bytes 614432 | tf_op jit(solution)/shard_map/ppermute | solution.py:240
  361.6 6.6 %collective-permute-done.13 = bf16[96,3200]{1,0:T(8,128)(2,1)S(1)} collective-permute-done((bf16[96,3200]{1,0:T(8,128)(2,1)}, bf16[96,3200]{1,0:T(8,128)(2,1)S(1)}, u32[]{:S(2)}, u32[]{:S(2)}) %collective-permute-start.13) | collective-permute-done | bytes 614432 | tf_op jit(solution)/shard_map/ppermute | solution.py:240
  376.0 13.8 %collective-permute-done.22 = bf16[96,3200]{1,0:T(8,128)(2,1)S(1)} collective-permute-done((bf16[96,3200]{1,0:T(8,128)(2,1)S(1)}, bf16[96,3200]{1,0:T(8,128)(2,1)S(1)}, u32[]{:S(2)}, u32[]{:S(2)}) %collective-permute-start.22) | collective-permute-done | bytes 614432 | tf_op jit(solution)/shard_map/ppermute | solution.py:240
  391.8 7.2 %collective-permute-done.19 = bf16[96,3200]{1,0:T(8,128)(2,1)S(1)} collective-permute-done((bf16[96,3200]{1,0:T(8,128)(2,1)S(1)}, bf16[96,3200]{1,0:T(8,128)(2,1)S(1)}, u32[]{:S(2)}, u32[]{:S(2)}) %collective-permute-start.19) | collective-permute-done | bytes 614432 | tf_op jit(solution)/shard_map/ppermute | solution.py:240
  405.9 14.4 %collective-permute-done.28 = bf16[96,3200]{1,0:T(8,128)(2,1)S(1)} collective-permute-done((bf16[96,3200]{1,0:T(8,128)(2,1)S(1)}, bf16[96,3200]{1,0:T(8,128)(2,1)S(1)}, u32[]{:S(2)}, u32[]{:S(2)}) %collective-permute-start.28) | collective-permute-done | bytes 614432 | tf_op jit(solution)/shard_map/ppermute | solution.py:240
  421.0 12.1 %collective-permute-done.25 = bf16[96,3200]{1,0:T(8,128)(2,1)S(1)} collective-permute-done((bf16[96,3200]{1,0:T(8,128)(2,1)S(1)}, bf16[96,3200]{1,0:T(8,128)(2,1)S(1)}, u32[]{:S(2)}, u32[]{:S(2)}) %collective-permute-start.25) | collective-permute-done | bytes 614432 | tf_op jit(solution)/shard_map/ppermute | solution.py:240
  436.4 2.3 collective-permute-done.38
  438.8 4.1 fusion.178
  442.9 4.1 broadcast_select_fusion.1
  450.7 5.2 %fusion.174 = (f32[8,192]{1,0:T(8,128)}, f32[8,192,576]{2,1,0:T(8,128)}) fusion(s32[8,576]{1,0:T(8,128)} %pad_add_fusion, s32[8,192]{1,0:T(8,128)S(1)} %broadcast_in_dim.59, bf16[8,192,128]{2,1,0:T(8,128)(2,1)S(1)} %bitcast.125, bf16[8,192,128]{2,1,0:T(8,128)(2,1)} %bitcast.131, bf16[8,192,128]{2,1,0:T(8,128)(2,1)S(1)} %bitcast.123, ...), kind=kOutput, calls=%fused_computation.302 | convolution fusion | flops 234455616 | bytes 5142528 | tf_op jit(solution)/shard_map/sub | solution.py:74
  455.9 4.7 fusion.171
  460.6 3.1 fusion.76
  464.8 25.9 %all_to_all.10 = bf16[8,192,256]{2,1,0:T(8,128)(2,1)S(1)} all-to-all(bf16[8,192,256]{2,1,0:T(8,128)(2,1)S(1)} %pad_maximum_fusion.5), channel_id=1, replica_groups=mesh['grp'=4,'chip'=4,'core'=2] {'chip','core'}, dimensions={0} | all-to-all | bytes 1572864 | tf_op jit(solution)/shard_map/all_to_all | solution.py:374
  (250 shorter events, 86.1 us)
Async XLA Ops:
  0.6 294.0 %copy-start = (f32[256]{0:T(256)S(1)}, f32[256]{0:T(256)}, u32[]{:S(2)}) copy-start(f32[256]{0:T(256)} %param.14) | copy-start | bytes 3076
  12.6 8.5 %collective-permute-start = (bf16[768,3200]{1,0:T(8,128)(2,1)}, bf16[768,3200]{1,0:T(8,128)(2,1)S(1)}, u32[]{:S(2)}, u32[]{:S(2)}) collective-permute-start(bf16[768,3200]{1,0:T(8,128)(2,1)} %bitcast.5), channel_id=1, source_target_pairs={{0,1},{1,0},{2,3},{3,2},{4,5},{5,4},{6,7},{7,6},{8,9},{9,8},{10,11... | collective-permute-start | bytes 14745608 | tf_op jit(solution)/shard_map/ppermute | solution.py:41
  24.5 18.3 %collective-permute-start.26 = (bf16[96,3200]{1,0:T(8,128)(2,1)S(1)}, bf16[96,3200]{1,0:T(8,128)(2,1)}, u32[]{:S(2)}, u32[]{:S(2)}) collective-permute-start(bf16[96,3200]{1,0:T(8,128)(2,1)S(1)} %slice.379), channel_id=1, source_target_pairs={{0,2},{6,4},{1,3},{7,5},{8,10},{14,12},{9,11},{15,13},{16,18},{22,... | collective-permute-start | bytes 1843208 | tf_op jit(solution)/shard_map/ppermute | solution.py:240
  47.0 92.0 %copy-start.9 = (bf16[96,3200]{1,0:T(8,128)(2,1)}, bf16[96,3200]{1,0:T(8,128)(2,1)S(1)}, u32[]{:S(2)}) copy-start(bf16[96,3200]{1,0:T(8,128)(2,1)S(1)} %get-tuple-element.66) | copy-start | bytes 1843204
  47.0 30.6 %copy-start.25 = (s32[1,32]{1,0:T(1,128)S(1)}, s32[1,32]{1,0:T(1,128)}, u32[]{:S(2)}) copy-start(s32[1,32]{1,0:T(1,128)} %param.16) | copy-start | bytes 388
  47.0 19.8 %collective-permute-start.27 = (bf16[96,3200]{1,0:T(8,128)(2,1)S(1)}, bf16[96,3200]{1,0:T(8,128)(2,1)S(1)}, u32[]{:S(2)}, u32[]{:S(2)}) collective-permute-start(bf16[96,3200]{1,0:T(8,128)(2,1)S(1)} %get-tuple-element.66), channel_id=1, source_target_pairs={{2,4},{4,2},{3,5},{5,3},{10,12},{12,10},{11,13},{13,11},{18,20},{2... | collective-permute-start | bytes 1843208 | tf_op jit(solution)/shard_map/ppermute | solution.py:240
  47.7 21.9 %collective-permute-start.11 = (bf16[96,3200]{1,0:T(8,128)(2,1)}, bf16[96,3200]{1,0:T(8,128)(2,1)S(1)}, u32[]{:S(2)}, u32[]{:S(2)}) collective-permute-start(bf16[96,3200]{1,0:T(8,128)(2,1)} %get-tuple-element.71), channel_id=1, source_target_pairs={{0,2},{6,4},{1,3},{7,5},{8,10},{14,12},{9,11},{15,13},{16,18},{22,... | collective-permute-start | bytes 1843208 | tf_op jit(solution)/shard_map/ppermute | solution.py:240
  60.5 22.3 %collective-permute-start.14 = (bf16[96,3200]{1,0:T(8,128)(2,1)}, bf16[96,3200]{1,0:T(8,128)(2,1)}, u32[]{:S(2)}, u32[]{:S(2)}) collective-permute-start(bf16[96,3200]{1,0:T(8,128)(2,1)} %get-tuple-element.70), channel_id=1, source_target_pairs={{0,2},{6,4},{1,3},{7,5},{8,10},{14,12},{9,11},{15,13},{16,18},{22,... | collective-permute-start | bytes 1843208 | tf_op jit(solution)/shard_map/ppermute | solution.py:240
  62.6 33.3 %collective-permute-start.17 = (bf16[96,3200]{1,0:T(8,128)(2,1)}, bf16[96,3200]{1,0:T(8,128)(2,1)}, u32[]{:S(2)}, u32[]{:S(2)}) collective-permute-start(bf16[96,3200]{1,0:T(8,128)(2,1)} %get-tuple-element.69), channel_id=1, source_target_pairs={{0,2},{6,4},{1,3},{7,5},{8,10},{14,12},{9,11},{15,13},{16,18},{22,... | collective-permute-start | bytes 1843208 | tf_op jit(solution)/shard_map/ppermute | solution.py:240
  64.7 44.4 %collective-permute-start.20 = (bf16[96,3200]{1,0:T(8,128)(2,1)}, bf16[96,3200]{1,0:T(8,128)(2,1)}, u32[]{:S(2)}, u32[]{:S(2)}) collective-permute-start(bf16[96,3200]{1,0:T(8,128)(2,1)} %get-tuple-element.68), channel_id=1, source_target_pairs={{0,2},{6,4},{1,3},{7,5},{8,10},{14,12},{9,11},{15,13},{16,18},{22,... | collective-permute-start | bytes 1843208 | tf_op jit(solution)/shard_map/ppermute | solution.py:240
  66.8 72.2 %copy-start.11 = (bf16[96,3200]{1,0:T(8,128)(2,1)}, bf16[96,3200]{1,0:T(8,128)(2,1)S(1)}, u32[]{:S(2)}) copy-start(bf16[96,3200]{1,0:T(8,128)(2,1)S(1)} %collective-permute-done.27) | copy-start | bytes 1843204
  66.8 55.4 %collective-permute-start.23 = (bf16[96,3200]{1,0:T(8,128)(2,1)}, bf16[96,3200]{1,0:T(8,128)(2,1)}, u32[]{:S(2)}, u32[]{:S(2)}) collective-permute-start(bf16[96,3200]{1,0:T(8,128)(2,1)} %get-tuple-element.67), channel_id=1, source_target_pairs={{0,2},{6,4},{1,3},{7,5},{8,10},{14,12},{9,11},{15,13},{16,18},{22,... | collective-permute-start | bytes 1843208 | tf_op jit(solution)/shard_map/ppermute | solution.py:240
  69.6 63.8 %collective-permute-start.8 = (bf16[96,3200]{1,0:T(8,128)(2,1)}, bf16[96,3200]{1,0:T(8,128)(2,1)}, u32[]{:S(2)}, u32[]{:S(2)}) collective-permute-start(bf16[96,3200]{1,0:T(8,128)(2,1)} %get-tuple-element.72), channel_id=1, source_target_pairs={{0,2},{6,4},{1,3},{7,5},{8,10},{14,12},{9,11},{15,13},{16,18},{22,... | collective-permute-start | bytes 1843208 | tf_op jit(solution)/shard_map/ppermute | solution.py:240
  139.9 18.0 %collective-permute-start.1 = (bf16[1,128,256]{2,1,0:T(8,128)(2,1)S(1)}, bf16[1,128,256]{2,1,0:T(8,128)(2,1)S(1)}, u32[]{:S(2)}, u32[]{:S(2)}) collective-permute-start(bf16[1,128,256]{2,1,0:T(8,128)(2,1)S(1)} %get-tuple-element.96), channel_id=1, source_target_pairs={{0,8},{8,16},{16,24},{1,9},{9,17},{17,25},{2,10},{10,18},{18,26},{... | collective-permute-start | bytes 196616 | tf_op jit(solution)/shard_map/ppermute | solution.py:27
  143.3 116.7 %collective-permute-start.12 = (bf16[96,3200]{1,0:T(8,128)(2,1)}, bf16[96,3200]{1,0:T(8,128)(2,1)}, u32[]{:S(2)}, u32[]{:S(2)}) collective-permute-start(bf16[96,3200]{1,0:T(8,128)(2,1)} %get-tuple-element.60), channel_id=1, source_target_pairs={{2,4},{4,2},{3,5},{5,3},{10,12},{12,10},{11,13},{13,11},{18,20},{2... | collective-permute-start | bytes 1843208 | tf_op jit(solution)/shard_map/ppermute | solution.py:240
  145.1 140.5 %collective-permute-start.15 = (bf16[96,3200]{1,0:T(8,128)(2,1)}, bf16[96,3200]{1,0:T(8,128)(2,1)}, u32[]{:S(2)}, u32[]{:S(2)}) collective-permute-start(bf16[96,3200]{1,0:T(8,128)(2,1)} %get-tuple-element.61), channel_id=1, source_target_pairs={{2,4},{4,2},{3,5},{5,3},{10,12},{12,10},{11,13},{13,11},{18,20},{2... | collective-permute-start | bytes 1843208 | tf_op jit(solution)/shard_map/ppermute | solution.py:240
  146.6 139.8 %collective-permute-start.18 = (bf16[96,3200]{1,0:T(8,128)(2,1)}, bf16[96,3200]{1,0:T(8,128)(2,1)}, u32[]{:S(2)}, u32[]{:S(2)}) collective-permute-start(bf16[96,3200]{1,0:T(8,128)(2,1)} %get-tuple-element.62), channel_id=1, source_target_pairs={{2,4},{4,2},{3,5},{5,3},{10,12},{12,10},{11,13},{13,11},{18,20},{2... | collective-permute-start | bytes 1843208 | tf_op jit(solution)/shard_map/ppermute | solution.py:240
  148.1 199.0 %all-to-all-start = ((bf16[8,100,768]{2,1,0:T(8,128)(2,1)}), bf16[8,100,768]{2,1,0:T(8,128)(2,1)}, u32[]{:S(2)}, u32[]{:S(2)}) async-start(bf16[8,100,768]{2,1,0:T(8,128)(2,1)} %constant_dynamic-update-slice_fusion), calls=%async_computation | async-start | bytes 2555904 | tf_op jit(solution)/shard_map/all_to_all | solution.py:315
  156.6 6.4 %collective-permute-start.2 = (bf16[1,128,256]{2,1,0:T(8,128)(2,1)S(1)}, bf16[1,128,256]{2,1,0:T(8,128)(2,1)S(1)}, u32[]{:S(2)}, u32[]{:S(2)}) collective-permute-start(bf16[1,128,256]{2,1,0:T(8,128)(2,1)S(1)} %get-tuple-element.95), channel_id=1, source_target_pairs={{8,0},{16,8},{24,16},{9,1},{17,9},{25,17},{10,2},{18,10},{26,18},{... | collective-permute-start | bytes 196616 | tf_op jit(solution)/shard_map/ppermute | solution.py:27
  168.8 8.7 %collective-permute-start.3 = (bf16[66,1,256]{2,1,0:T(2,128)(2,1)S(1)}, bf16[66,1,256]{2,1,0:T(2,128)(2,1)S(1)}, u32[]{:S(2)}, u32[]{:S(2)}) collective-permute-start(bf16[66,1,256]{2,1,0:T(2,128)(2,1)S(1)} %get-tuple-element.90), channel_id=1, source_target_pairs={{0,1},{1,2},{2,3},{3,4},{4,5},{5,6},{6,7},{8,9},{9,10},{10,11},{11... | collective-permute-start | bytes 101384 | tf_op jit(solution)/shard_map/ppermute | solution.py:27
  170.4 8.6 %collective-permute-start.4 = (bf16[66,1,256]{2,1,0:T(2,128)(2,1)S(1)}, bf16[66,1,256]{2,1,0:T(2,128)(2,1)S(1)}, u32[]{:S(2)}, u32[]{:S(2)}) collective-permute-start(bf16[66,1,256]{2,1,0:T(2,128)(2,1)S(1)} %get-tuple-element.91), channel_id=1, source_target_pairs={{1,0},{2,1},{3,2},{4,3},{5,4},{6,5},{7,6},{9,8},{10,9},{11,10},{12... | collective-permute-start | bytes 101384 | tf_op jit(solution)/shard_map/ppermute | solution.py:27
  177.5 108.9 %collective-permute-start.21 = (bf16[96,3200]{1,0:T(8,128)(2,1)}, bf16[96,3200]{1,0:T(8,128)(2,1)}, u32[]{:S(2)}, u32[]{:S(2)}) collective-permute-start(bf16[96,3200]{1,0:T(8,128)(2,1)} %get-tuple-element.63), channel_id=1, source_target_pairs={{2,4},{4,2},{3,5},{5,3},{10,12},{12,10},{11,13},{13,11},{18,20},{2... | collective-permute-start | bytes 1843208 | tf_op jit(solution)/shard_map/ppermute | solution.py:240
  179.0 82.6 %collective-permute-start.5 = (bf16[96,3200]{1,0:T(8,128)(2,1)}, bf16[96,3200]{1,0:T(8,128)(2,1)}, u32[]{:S(2)}, u32[]{:S(2)}) collective-permute-start(bf16[96,3200]{1,0:T(8,128)(2,1)} %get-tuple-element.16), channel_id=1, source_target_pairs={{0,2},{6,4},{1,3},{7,5},{8,10},{14,12},{9,11},{15,13},{16,18},{22,... | collective-permute-start | bytes 1843208 | tf_op jit(solution)/shard_map/ppermute | solution.py:240
  254.5 32.0 %slice-start = ((s8[4915200]{0:T(1024)(128)(4,1)}), s8[4194304]{0:T(1024)(128)(4,1)S(1)}, s32[]{:S(2)}) async-start(s8[4915200]{0:T(1024)(128)(4,1)} %bitcast.107), calls=%async_computation.2 | async-start | bytes 8388608
  260.1 26.4 %collective-permute-start.24 = (bf16[96,3200]{1,0:T(8,128)(2,1)}, bf16[96,3200]{1,0:T(8,128)(2,1)}, u32[]{:S(2)}, u32[]{:S(2)}) collective-permute-start(bf16[96,3200]{1,0:T(8,128)(2,1)} %get-tuple-element.64), channel_id=1, source_target_pairs={{2,4},{4,2},{3,5},{5,3},{10,12},{12,10},{11,13},{13,11},{18,20},{2... | collective-permute-start | bytes 1843208 | tf_op jit(solution)/shard_map/ppermute | solution.py:240
  261.6 24.9 %collective-permute-start.9 = (bf16[96,3200]{1,0:T(8,128)(2,1)}, bf16[96,3200]{1,0:T(8,128)(2,1)}, u32[]{:S(2)}, u32[]{:S(2)}) collective-permute-start(bf16[96,3200]{1,0:T(8,128)(2,1)} %get-tuple-element.59), channel_id=1, source_target_pairs={{2,4},{4,2},{3,5},{5,3},{10,12},{12,10},{11,13},{13,11},{18,20},{2... | collective-permute-start | bytes 1843208 | tf_op jit(solution)/shard_map/ppermute | solution.py:240
  285.6 5.2 %collective-permute-start.6 = (bf16[96,3200]{1,0:T(8,128)(2,1)S(1)}, bf16[96,3200]{1,0:T(8,128)(2,1)S(1)}, u32[]{:S(2)}, u32[]{:S(2)}) collective-permute-start(bf16[96,3200]{1,0:T(8,128)(2,1)S(1)} %add.321), channel_id=1, source_target_pairs={{2,4},{4,2},{3,5},{5,3},{10,12},{12,10},{11,13},{13,11},{18,20},{2... | collective-permute-start | bytes 1843208 | tf_op jit(solution)/shard_map/ppermute | solution.py:240
  290.8 48.0 %collective-permute-start.10 = (bf16[96,3200]{1,0:T(8,128)(2,1)}, bf16[96,3200]{1,0:T(8,128)(2,1)S(1)}, u32[]{:S(2)}, u32[]{:S(2)}) collective-permute-start(bf16[96,3200]{1,0:T(8,128)(2,1)} %get-tuple-element.18), channel_id=1, source_target_pairs={{4,6},{2,0},{5,7},{3,1},{12,14},{10,8},{13,15},{11,9},{20,22},{18,... | collective-permute-start | bytes 1843208 | tf_op jit(solution)/shard_map/ppermute | solution.py:240
  293.4 46.8 %collective-permute-start.7 = (bf16[96,3200]{1,0:T(8,128)(2,1)S(1)}, bf16[96,3200]{1,0:T(8,128)(2,1)S(1)}, u32[]{:S(2)}, u32[]{:S(2)}) collective-permute-start(bf16[96,3200]{1,0:T(8,128)(2,1)S(1)} %add.323), channel_id=1, source_target_pairs={{4,6},{2,0},{5,7},{3,1},{12,14},{10,8},{13,15},{11,9},{20,22},{18,... | collective-permute-start | bytes 1843208 | tf_op jit(solution)/shard_map/ppermute | solution.py:240
  301.8 43.7 %copy-start.7 = (f32[1,8192]{1,0:T(1,128)}, f32[1,8192]{1,0:T(1,128)S(1)}, u32[]{:S(2)}) copy-start(f32[1,8192]{1,0:T(1,128)S(1)} %fusion.177) | copy-start | bytes 98308
  301.8 42.6 %copy-start.14 = (f32[3200]{0:T(1024)S(1)}, f32[3200]{0:T(1024)}, u32[]{:S(2)}) copy-start(f32[3200]{0:T(1024)} %param.20) | copy-start | bytes 38404
  338.9 19.0 %collective-permute-start.16 = (bf16[96,3200]{1,0:T(8,128)(2,1)}, bf16[96,3200]{1,0:T(8,128)(2,1)}, u32[]{:S(2)}, u32[]{:S(2)}) collective-permute-start(bf16[96,3200]{1,0:T(8,128)(2,1)} %get-tuple-element.20), channel_id=1, source_target_pairs={{4,6},{2,0},{5,7},{3,1},{12,14},{10,8},{13,15},{11,9},{20,22},{18,... | collective-permute-start | bytes 1843208 | tf_op jit(solution)/shard_map/ppermute | solution.py:240
  340.2 28.0 %collective-permute-start.13 = (bf16[96,3200]{1,0:T(8,128)(2,1)}, bf16[96,3200]{1,0:T(8,128)(2,1)S(1)}, u32[]{:S(2)}, u32[]{:S(2)}) collective-permute-start(bf16[96,3200]{1,0:T(8,128)(2,1)} %get-tuple-element.19), channel_id=1, source_target_pairs={{4,6},{2,0},{5,7},{3,1},{12,14},{10,8},{13,15},{11,9},{20,22},{18,... | collective-permute-start | bytes 1843208 | tf_op jit(solution)/shard_map/ppermute | solution.py:240
  346.6 27.0 %collective-permute-start.33 = (bf16[96,3200]{1,0:T(8,128)(2,1)S(1)}, bf16[96,3200]{1,0:T(8,128)(2,1)}, u32[]{:S(2)}, u32[]{:S(2)}) collective-permute-start(bf16[96,3200]{1,0:T(8,128)(2,1)S(1)} %get-tuple-element.39), channel_id=1, source_target_pairs={{0,1},{1,0},{2,3},{3,2},{4,5},{5,4},{6,7},{7,6},{8,9},{9,8},{10,11... | collective-permute-start | bytes 1843208 | tf_op jit(solution)/shard_map/ppermute | solution.py:41
  346.6 24.6 %collective-permute-start.32 = (bf16[96,3200]{1,0:T(8,128)(2,1)S(1)}, bf16[96,3200]{1,0:T(8,128)(2,1)}, u32[]{:S(2)}, u32[]{:S(2)}) collective-permute-start(bf16[96,3200]{1,0:T(8,128)(2,1)S(1)} %get-tuple-element.41), channel_id=1, source_target_pairs={{0,1},{1,0},{2,3},{3,2},{4,5},{5,4},{6,7},{7,6},{8,9},{9,8},{10,11... | collective-permute-start | bytes 1843208 | tf_op jit(solution)/shard_map/ppermute | solution.py:41
  348.5 56.3 %collective-permute-start.29 = (bf16[800,768]{1,0:T(8,128)(2,1)S(1)}, bf16[800,768]{1,0:T(8,128)(2,1)S(1)}, u32[]{:S(2)}, u32[]{:S(2)}) collective-permute-start(bf16[800,768]{1,0:T(8,128)(2,1)S(1)} %reshape.330), channel_id=1, source_target_pairs={{0,8},{8,16},{16,24},{24,0},{1,9},{9,17},{17,25},{25,1},{2,10},{10... | collective-permute-start | bytes 3686408 | tf_op jit(solution)/shard_map/ppermute | solution.py:321
  357.9 47.7 %collective-permute-start.30 = (bf16[800,768]{1,0:T(8,128)(2,1)S(1)}, bf16[800,768]{1,0:T(8,128)(2,1)S(1)}, u32[]{:S(2)}, u32[]{:S(2)}) collective-permute-start(bf16[800,768]{1,0:T(8,128)(2,1)S(1)} %reshape.330), channel_id=1, source_target_pairs={{0,16},{8,24},{16,0},{24,8},{1,17},{9,25},{17,1},{25,9},{2,18},{10... | collective-permute-start | bytes 3686408 | tf_op jit(solution)/shard_map/ppermute | solution.py:321
  368.2 37.6 %collective-permute-start.31 = (bf16[800,768]{1,0:T(8,128)(2,1)S(1)}, bf16[800,768]{1,0:T(8,128)(2,1)S(1)}, u32[]{:S(2)}, u32[]{:S(2)}) collective-permute-start(bf16[800,768]{1,0:T(8,128)(2,1)S(1)} %reshape.330), channel_id=1, source_target_pairs={{0,24},{8,0},{16,8},{24,16},{1,25},{9,1},{17,9},{25,17},{2,26},{10... | collective-permute-start | bytes 3686408 | tf_op jit(solution)/shard_map/ppermute | solution.py:321
  371.2 18.7 %collective-permute-start.22 = (bf16[96,3200]{1,0:T(8,128)(2,1)S(1)}, bf16[96,3200]{1,0:T(8,128)(2,1)S(1)}, u32[]{:S(2)}, u32[]{:S(2)}) collective-permute-start(bf16[96,3200]{1,0:T(8,128)(2,1)S(1)} %copy-done.20), channel_id=1, source_target_pairs={{4,6},{2,0},{5,7},{3,1},{12,14},{10,8},{13,15},{11,9},{20,22},{18,... | collective-permute-start | bytes 1843208 | tf_op jit(solution)/shard_map/ppermute | solution.py:240
  373.6 25.5 %collective-permute-start.19 = (bf16[96,3200]{1,0:T(8,128)(2,1)S(1)}, bf16[96,3200]{1,0:T(8,128)(2,1)S(1)}, u32[]{:S(2)}, u32[]{:S(2)}) collective-permute-start(bf16[96,3200]{1,0:T(8,128)(2,1)S(1)} %copy-done.19), channel_id=1, source_target_pairs={{4,6},{2,0},{5,7},{3,1},{12,14},{10,8},{13,15},{11,9},{20,22},{18,... | collective-permute-start | bytes 1843208 | tf_op jit(solution)/shard_map/ppermute | solution.py:240
  389.9 13.3 %collective-permute-start.35 = (bf16[96,3200]{1,0:T(8,128)(2,1)S(1)}, bf16[96,3200]{1,0:T(8,128)(2,1)S(1)}, u32[]{:S(2)}, u32[]{:S(2)}) collective-permute-start(bf16[96,3200]{1,0:T(8,128)(2,1)S(1)} %get-tuple-element.35), channel_id=1, source_target_pairs={{0,1},{1,0},{2,3},{3,2},{4,5},{5,4},{6,7},{7,6},{8,9},{9,8},{10,11... | collective-permute-start | bytes 1843208 | tf_op jit(solution)/shard_map/ppermute | solution.py:41
  399.1 2.6 collective-permute-start.34
  401.7 18.5 %collective-permute-start.28 = (bf16[96,3200]{1,0:T(8,128)(2,1)S(1)}, bf16[96,3200]{1,0:T(8,128)(2,1)S(1)}, u32[]{:S(2)}, u32[]{:S(2)}) collective-permute-start(bf16[96,3200]{1,0:T(8,128)(2,1)S(1)} %copy-done.17), channel_id=1, source_target_pairs={{4,6},{2,0},{5,7},{3,1},{12,14},{10,8},{13,15},{11,9},{20,22},{18,... | collective-permute-start | bytes 1843208 | tf_op jit(solution)/shard_map/ppermute | solution.py:240
  403.1 29.9 %collective-permute-start.25 = (bf16[96,3200]{1,0:T(8,128)(2,1)S(1)}, bf16[96,3200]{1,0:T(8,128)(2,1)S(1)}, u32[]{:S(2)}, u32[]{:S(2)}) collective-permute-start(bf16[96,3200]{1,0:T(8,128)(2,1)S(1)} %copy-done.18), channel_id=1, source_target_pairs={{4,6},{2,0},{5,7},{3,1},{12,14},{10,8},{13,15},{11,9},{20,22},{18,... | collective-permute-start | bytes 1843208 | tf_op jit(solution)/shard_map/ppermute | solution.py:240
  404.9 31.5 %collective-permute-start.37 = (bf16[96,3200]{1,0:T(8,128)(2,1)S(1)}, bf16[96,3200]{1,0:T(8,128)(2,1)S(1)}, u32[]{:S(2)}, u32[]{:S(2)}) collective-permute-start(bf16[96,3200]{1,0:T(8,128)(2,1)S(1)} %get-tuple-element.31), channel_id=1, source_target_pairs={{0,1},{1,0},{2,3},{3,2},{4,5},{5,4},{6,7},{7,6},{8,9},{9,8},{10,11... | collective-permute-start | bytes 1843208 | tf_op jit(solution)/shard_map/ppermute | solution.py:41
  405.6 30.7 %collective-permute-start.36 = (bf16[96,3200]{1,0:T(8,128)(2,1)S(1)}, bf16[96,3200]{1,0:T(8,128)(2,1)S(1)}, u32[]{:S(2)}, u32[]{:S(2)}) collective-permute-start(bf16[96,3200]{1,0:T(8,128)(2,1)S(1)} %get-tuple-element.33), channel_id=1, source_target_pairs={{0,1},{1,0},{2,3},{3,2},{4,5},{5,4},{6,7},{7,6},{8,9},{9,8},{10,11... | collective-permute-start | bytes 1843208 | tf_op jit(solution)/shard_map/ppermute | solution.py:41
  435.7 3.1 collective-permute-start.39
  435.8 2.9 collective-permute-start.38
  (25 other events, 251.8 us)

commit v3 on v2

--- a/solution.py
+++ b/solution.py
@@ -1,8 +1,11 @@
+import functools
 import math
 
 import jax
 import jax.numpy as jnp
 from jax import lax
+from jax.experimental import pallas as pl
+from jax.experimental.pallas import tpu as pltpu
 from jax.sharding import Mesh
 from jax.sharding import PartitionSpec as P
 
@@ -220,30 +223,167 @@
     return jnp.sum(jnp.where(earlier, counts[None, :], 0), axis=1)
 
 
-def hop_pairs(hop, chips):
-    return [(hop, hop + 1), (chips - 1 - hop, chips - 2 - hop)]
-
-
-def merge_line(chunks, chips):
-    total = list(chunks)
-    got = [None] * len(chunks)
-    waves = []
-    for step in range(len(chunks) + chips - 2):
-        arrived = []
-        for hop in reversed(range(chips - 1)):
-            at = step - hop
-            if not 0 <= at < len(chunks):
-                continue
-            load = chunks[at] if hop == 0 else chunks[at] + got[at]
-            if len(waves) >= 2:
-                load, waves[-2] = lax.optimization_barrier((load, waves[-2]))
-            fresh = lax.ppermute(load, "chip", hop_pairs(hop, chips))
-            arrived.append((at, fresh))
-        for at, fresh in arrived:
-            got[at] = fresh
-            total[at] = total[at] + fresh
-        waves.append([fresh for _, fresh in arrived])
-    return total
+def merge_kernel(chips, chunks, rows, own, weight, gain, mixed, *scratch):
+    right_in, left_in, normed, tile, r_send, r_recv, l_send, l_recv, c_send, c_recv = scratch
+    chip, core = lax.axis_index("chip"), lax.axis_index("core")
+    half = chunks * rows
+    last = chips - 1
+    nxt, prv = lax.rem(chip + 1, chips), lax.rem(chip + chips - 1, chips)
+    mesh_id = pl.DeviceIdType.MESH
+
+    barrier = pltpu.get_barrier_semaphore()
+    pl.semaphore_signal(barrier, inc=1, device_id={"core": 1 - core}, device_id_type=mesh_id)
+
+    @pl.when(chip > 0)
+    def _():
+        pl.semaphore_signal(barrier, inc=1, device_id={"chip": prv}, device_id_type=mesh_id)
+
+    @pl.when(chip < last)
+    def _():
+        pl.semaphore_signal(barrier, inc=1, device_id={"chip": nxt}, device_id_type=mesh_id)
+
+    inner = (chip > 0) & (chip < last)
+
+    @pl.when(inner)
+    def _():
+        pl.semaphore_wait(barrier, 3)
+
+    @pl.when(jnp.logical_not(inner))
+    def _():
+        pl.semaphore_wait(barrier, 2)
+
+    def span(c):
+        return pl.ds(pl.multiple_of(c * rows, rows), rows)
+
+    def to_right(c, source):
+        return pltpu.make_async_remote_copy(
+            source.at[span(c)], right_in.at[span(c)], r_send.at[c], r_recv.at[c],
+            device_id={"chip": nxt}, device_id_type=mesh_id,
+        )
+
+    def to_left(c, source):
+        return pltpu.make_async_remote_copy(
+            source.at[span(c)], left_in.at[span(c)], l_send.at[c], l_recv.at[c],
+            device_id={"chip": prv}, device_id_type=mesh_id,
+        )
+
+    def core_span(c, which):
+        return pl.ds(pl.multiple_of(which * half + c * rows, rows), rows)
+
+    def to_core(c):
+        there = normed.at[core_span(c, core)]
+        return pltpu.make_async_remote_copy(
+            there, there, c_send.at[c], c_recv.at[c],
+            device_id={"core": 1 - core}, device_id_type=mesh_id,
+        )
+
+    def each(body):
+        def step(c, carry):
+            body(c)
+            return carry
+
+        lax.fori_loop(0, chunks, step, 0)
+
+    @pl.when(chip == 0)
+    def _():
+        each(lambda c: to_right(c, own).start())
+
+    @pl.when(chip == last)
+    def _():
+        each(lambda c: to_left(c, own).start())
+
+    def project(at):
+        mixed[at] = jnp.dot(normed[at], weight[...], preferred_element_type=jnp.float32)
+
+    def far(c):
+        to_core(c).wait_recv()
+        project(core_span(c, 1 - core))
+
+    def step(c):
+        at = span(c)
+
+        @pl.when(chip > 0)
+        def _():
+            to_right(c, right_in).wait_recv()
+            right_in[at] = right_in[at] + own[at]
+
+            @pl.when(chip < last)
+            def _():
+                to_right(c, right_in).start()
+
+        @pl.when(chip == 0)
+        def _():
+            right_in[at] = own[at]
+
+        @pl.when(chip < last)
+        def _():
+            to_left(c, left_in).wait_recv()
+            tile[...] = right_in[at] + left_in[at]
+
+            @pl.when(chip > 0)
+            def _():
+                left_in[at] = left_in[at] + own[at]
+                to_left(c, left_in).start()
+
+        @pl.when(chip == last)
+        def _():
+            tile[...] = right_in[at]
+
+        normed[core_span(c, core)] = layer_norm(tile[...], gain[...])
+        to_core(c).start()
+        project(core_span(c, core))
+
+        @pl.when(c > 0)
+        def _():
+            far(c - 1)
+
+    each(step)
+    far(chunks - 1)
+    each(lambda c: to_core(c).wait_send())
+
+    @pl.when(chip < last)
+    def _():
+        each(lambda c: to_right(c, right_in).wait_send())
+
+    @pl.when(chip > 0)
+    def _():
+        each(lambda c: to_left(c, left_in).wait_send())
+
+
+def merge_project(own, weight, gain, chips, chunks):
+    half, width = own.shape
+    columns = weight.shape[1]
+    rows = half // chunks
+    vmem = pl.BlockSpec(memory_space=pltpu.VMEM)
+    sems = pltpu.SemaphoreType.DMA((chunks,))
+    return pl.pallas_call(
+        functools.partial(merge_kernel, chips, chunks, rows),
+        out_shape=jax.ShapeDtypeStruct((2 * half, columns), jnp.float32),
+        in_specs=[vmem] * 3,
+        out_specs=vmem,
+        scratch_shapes=[
+            pltpu.VMEM((half, width), jnp.bfloat16),
+            pltpu.VMEM((half, width), jnp.bfloat16),
+            pltpu.VMEM((2 * half, width), jnp.bfloat16),
+            pltpu.VMEM((rows, width), jnp.bfloat16),
+        ]
+        + [sems] * 6,
+        compiler_params=pltpu.CompilerParams(
+            collective_id=0, has_side_effects=True, vmem_limit_bytes=50 * 2**20
+        ),
+        cost_estimate=pl.CostEstimate(
+            flops=4 * half * width * columns, bytes_accessed=400 * 2**20, transcendentals=0
+        ),
+    )(own, weight, gain.reshape(1, width))
+
+
+def sum_over_dev(value, chips):
+    value = value + swap_core(value)
+    shift = 1
+    while shift < chips:
+        value = value + lax.ppermute(value, "chip", [(i, i ^ shift) for i in range(chips)])
+        shift *= 2
+    return value
 
 
 def shards_by_head(
@@ -299,19 +439,14 @@
             "ps,std->ptd", mask, tile_tokens, preferred_element_type=jnp.float32
         ).astype(jnp.bfloat16)
 
-    n_chunks = 8
-    per_chunk = half // n_chunks
     given = pick(other_mask).reshape(half * tile_len, model_width)
     kept = pick(mine_mask).reshape(half * tile_len, model_width)
     chip_half = kept + swap_core(given)
-    chunk_rows = per_chunk * tile_len
-    chunks = [chip_half[i * chunk_rows : (i + 1) * chunk_rows] for i in range(n_chunks)]
 
     split = qkv_weight.reshape(rows_here, 3, HEADS, HD)
     send_weight = jnp.stack(
         [split[:, :, h : h + each].reshape(rows_here, 3 * wide) for h in first_head], axis=0
     )
-    chunks[0], send_weight = lax.optimization_barrier((chunks[0], send_weight))
     block = lax.all_to_all(send_weight, dev, split_axis=0, concat_axis=0, tiled=True)
     block = block.reshape(holders * rows_here, 3 * wide)
     group_rows = holders * rows_here
@@ -323,26 +458,17 @@
             weights, far, ((group - shift) % groups) * group_rows, 0
         )
 
-    canvas, chunks[0] = lax.optimization_barrier((canvas, chunks[0]))
+    canvas, send_weight = lax.optimization_barrier((canvas, send_weight))
     height, breadth = canvas.shape[0], canvas.shape[1]
     padded = with_halo(with_halo(canvas, "grp", 0), dev, 1)
     score_flat = conv_scores(padded, conv_weight, conv_bias, score_weight, height, breadth)
     score_map = score_flat.reshape(height, breadth)
     tile_score = jnp.take(score_flat, tile_cell[0]).astype(jnp.bfloat16)
     own_scores = jnp.sum(source.astype(jnp.float32) * tile_score.astype(jnp.float32), axis=1)
-    held_score = lax.psum(own_scores, dev)
+    held_score = sum_over_dev(own_scores, chips)
     sharpness = jnp.repeat(0.5 + jax.nn.softplus(held_score), tile_len)
 
-    merged = merge_line(chunks, chips)
-    normed = [layer_norm(rows, ln_gain) for rows in merged]
-    far = [swap_core(rows) for rows in normed]
-    near_half, far_half = jnp.concatenate(normed, axis=0), jnp.concatenate(far, axis=0)
-    near_mixed = jnp.dot(near_half, weights, preferred_element_type=jnp.float32)
-    far_mixed = jnp.dot(far_half, weights, preferred_element_type=jnp.float32)
-    mixed = jnp.concatenate(
-        [jnp.where(core == 0, near_mixed, far_mixed), jnp.where(core == 0, far_mixed, near_mixed)],
-        axis=0,
-    )
+    mixed = merge_project(chip_half, weights, ln_gain, chips, 8)
     queries = mixed[:, :wide].astype(jnp.bfloat16)
     keys = (mixed[:, wide : 2 * wide] * sharpness[:, None]).astype(jnp.bfloat16)
     values = mixed[:, 2 * wide :].astype(jnp.bfloat16)
@@ -400,7 +526,7 @@
         P(every, None),
     )
     return jax.shard_map(
-        shards_by_head if devs <= HEADS else shards_by_core,
+        shards_by_head if devs == 8 else shards_by_core,
         mesh=fine,
         in_specs=placed,
         out_specs=(P("grp", dev), P(every, None)),

time: 502 us -> 425 us (0.85)
  Pallas kernels: 0 us -> 218 us
  waiting for transfers between devices: 141 us -> 17.2 us
  starting transfers between devices: 121 us -> 28.4 us
  blocking collectives: 61.9 us -> 23.4 us
  other arithmetic: 70.2 us -> 34.8 us
  matrix products: 68 us -> 61.9 us
  local copies, waits for them, and re-layouts: 27.9 us -> 33.5 us
    pallas_call x0 -> x1, Pallas kernels: none -> 218 us  [merge_project(): pl.pallas_call(functools.partial(merge_kernel, chips, chunks, rows), out_...]
    ppermute x24 -> x2, waiting for transfers between devices: 128 us -> 2.04 us  [sum_over_dev(): lax.ppermute(value, 'chip', [(i, i ^ shift) for i in range(chips)])]
    ppermute x24 -> x2, starting transfers between devices: 99.1 us -> 5.19 us  [sum_over_dev(): lax.ppermute(value, 'chip', [(i, i ^ shift) for i in range(chips)])]
    psum x1 -> x0, blocking collectives: 35.9 us -> none  [shards_by_head(): held_score = lax.psum(own_scores, dev)]
    add x5 -> x2, other arithmetic: 16.8 us -> 0.01 us  [the longest x1 0.01 us: sum_over_dev(): value = value + swap_core(value)]
    ppermute x3, waiting for transfers between devices: 0.01 us -> 14.4 us  [shards_by_head(): lax.ppermute(block, 'grp', [(i, (i + shift) % groups) for i in range(grou...]
    reduce_sum x16 -> x0, other arithmetic: 13.5 us -> none  [the longest x8 10.9 us: layer_norm(): center = jnp.mean(values, axis=1, keepdims=True)]
    concatenate x2, other arithmetic: 28.3 us -> 18.1 us  [with_halo(): return jnp.concatenate([before, value, after], axis=dim)]
  transfers between devices with their start and end apart: 41 -> 12, of which waited for: 16 -> 3; matrix products, arithmetic and copies ran while one was open for 23% -> 21% of each run, Pallas kernels for 0% -> 0%
where the time goes in v3:
time: 425 us; the launch traced here: 418 us
  Pallas kernels  218 us (51%)
  matrix products  61.9 us (15%)
  other arithmetic  34.8 us (8%)
  local copies, waits for them, and re-layouts  33.5 us (8%)
  starting transfers between devices  28.4 us (7%)
  blocking collectives  23.4 us (6%)
  waiting for transfers between devices  17.2 us (4%)
    pallas_call x1, Pallas kernels, merge_project(): pl.pallas_call(functools.partial(merge_kernel, chips, chunks, rows), out_...  218 us
    dot_general x9, matrix products, conv_scores(): jnp.dot(window, conv_weight[offset:offset + channels], preferred_element_...  31.2 us
    all_to_all x1, blocking collectives, shards_by_head(): lax.all_to_all(mine, dev, split_axis=0, concat_axis=0, tiled=True)  23.4 us
    concatenate x2, other arithmetic, with_halo(): return jnp.concatenate([before, value, after], axis=dim)  18.1 us
    ppermute x3, waiting for transfers between devices, shards_by_head(): lax.ppermute(block, 'grp', [(i, (i + shift) % groups) for i in range(grou...  14.4 us
    unnamed x53, local copies, waits for them, and re-layouts  10.1 us
    dot_general x2, matrix products, pick(): jnp.einsum('ps,std->ptd', mask, tile_tokens, preferred_element_type=jnp.f...  9.92 us
    sub x2, matrix products, attend(): weights = jnp.exp(logits - peak)  9.77 us
  transfers between devices with their start and end apart: 12, of which 3 were waited for; matrix products, arithmetic and copies ran while one was open for 21% of the time, Pallas kernels for 0%

profile of v3, /device:TPU:0, one launch (start us, length us, event | category | flops | bytes accessed | tf_op | source)
XLA Modules:
  0.0 418.4 jit_solution(3610669615267436794)
XLA Ops:
  0.6 2.4 reshape.223
  9.9 6.3 %all-to-all-start = ((bf16[8,100,768]{2,1,0:T(8,128)(2,1)}), bf16[8,100,768]{2,1,0:T(8,128)(2,1)S(1)}, u32[]{:S(2)}, u32[]{:S(2)}) async-start(bf16[8,100,768]{2,1,0:T(8,128)(2,1)} %constant_dynamic-update-slice_fusion), calls=%async_computation | async-start | bytes 2555904 | tf_op jit(solution)/shard_map/all_to_all | solution.py:450
  16.2 0.9 fusion.115
  17.1 3.4 collective-permute-start
  20.5 1.3 collective-permute-start.1
  24.2 3.9 convolution_convert_fusion
  28.1 3.6 copy.24
  31.9 6.1 %convolution_convert_fusion.1 = bf16[32,24,3200]{2,0,1:T(8,128)(2,1)} fusion(bf16[32,24,3200]{2,1,0:T(8,128)(2,1)} %param.15, pred[]{:T(512)S(6)} %eq.32, bf16[64,32]{1,0:T(8,128)(2,1)S(1)} %fusion.83), kind=kOutput, calls=%fused_computation.21 | convolution fusion | flops 159745024 | bytes 9834497 | tf_op jit(solution)/shard_map/ps,std->ptd/dot_general | solution.py:438
  40.5 5.7 %pad_maximum_fusion.3 = (bf16[64,128,256]{2,1,0:T(8,128)(2,1)S(1)}, bf16[64,128,256]{2,1,0:T(8,128)(2,1)S(1)}, bf16[66,128,256]{2,1,0:T(8,128)(2,1)S(1)}) fusion(bf16[64,128,256]{2,1,0:T(8,128)(2,1)} %param.11, bf16[1,128,256]{2,1,0:T(8,128)(2,1)S(1)} %collective-permute-done, bf16[1,128,256]{2,1,0:T(8,128)(2,1)S(1)} %collective-permute-done.1, ...), kind=kLoop, calls=%fused_computation.38 | loop fusion | flops 16777216 | bytes 16908288 | tf_op jit(solution)/shard_map/concatenate | solution.py:40
  46.4 2.2 collective-permute-start.2
  48.6 1.5 collective-permute-start.3
  50.0 1.2 fusion.73
  51.3 4.5 %fusion.66 = f32[8192,256]{1,0:T(8,128)} fusion(bf16[8192,256]{1,0:T(8,128)(2,1)S(1)} %bitcast.108, bf16[2304,256]{1,0:T(8,128)(2,1)S(1)} %copy-done.8), kind=kOutput, calls=%fused_computation.93 | convolution fusion | flops 1073741824 | bytes 12713984 | tf_op jit(solution)/shard_map/dot_general | solution.py:63
  55.8 12.4 %pad_maximum_fusion.2 = (bf16[64,128,256]{2,1,0:T(8,128)(2,1)}, bf16[64,128,256]{2,1,0:T(8,128)(2,1)S(1)}, bf16[64,128,256]{2,1,0:T(8,128)(2,1)}, bf16[64,128,25...) fusion(bf16[66,128,256]{2,1,0:T(8,128)(2,1)S(1)} %constant_dynamic-update-slice_fusion.8, ...), kind=kLoop, calls=%fused_computation.37 | loop fusion | flops 50331648 | bytes 29558784 | tf_op jit(solution)/shard_map/concatenate | solution.py:40
  68.2 1.2 convolution_add_fusion.5
  69.5 0.9 copy-done.4
  70.4 1.3 convolution_add_fusion.4
  71.7 0.9 copy-done.3
  72.6 1.3 convolution_add_fusion.3
  73.9 0.9 copy-done.5
  74.8 4.5 %fusion.64 = f32[8192,256]{1,0:T(8,128)} fusion(bf16[8192,256]{1,0:T(8,128)(2,1)S(1)} %bitcast.110, bf16[2304,256]{1,0:T(8,128)(2,1)S(1)} %copy-done.8), kind=kOutput, calls=%fused_computation.91 | convolution fusion | flops 1073741824 | bytes 12713984 | tf_op jit(solution)/shard_map/dot_general | solution.py:63
  79.3 1.2 convolution_add_fusion.2
  80.5 0.9 copy-done.2
  81.5 4.5 %convolution_add_fusion.1 = f32[8192,256]{1,0:T(8,128)} fusion(f32[8192,256]{1,0:T(8,128)S(1)} %convolution_add_fusion.2, bf16[8192,256]{1,0:T(8,128)(2,1)S(1)} %bitcast.104, bf16[2304,256]{1,0:T(8,128)(2,1)S(1)} %copy-done.8), kind=kOutput, calls=%fused_computation.6 | convolution fusion | flops 1075838976 | bytes 21102592 | tf_op jit(solution)/shard_map/dot_general | solution.py:63
  86.2 2.9 collective-permute-start.5
  89.1 11.5 %fusion.11 = f32[8192,256]{1,0:T(8,128)S(1)} fusion(f32[8192,256]{1,0:T(8,128)} %fusion.64, f32[8192,256]{1,0:T(8,128)} %fusion.66, f32[8192,256]{1,0:T(8,128)} %convolution_add_fusion.1, bf16[8192,256]{1,0:T(8,128)(2,1)} %bitcast.111, f32[256]{0:T(256)S(1)} %copy-done.12, bf16[2304,256]{1,0:T(8,128)(2,1)} %param.12), kind=kOutput, calls=%fused_computation.19 | convolution fusion | flops 1098907648 | bytes 37880832 | tf_op jit(solution)/shard_map/dot_general | solution.py:63
  100.6 1.6 collective-permute-start.6
  102.2 2.3 collective-permute-start.7
  104.5 7.1 %fusion.125 = f32[1,8192]{1,0:T(1,128)S(1)} fusion(f32[8192,256]{1,0:T(8,128)S(1)} %fusion.11, f32[256,1]{0,1:T(1,128)S(1)} %bitcast.102), kind=kOutput, calls=%fused_computation.185 | convolution fusion | flops 25165824 | bytes 8422400 | tf_op jit(solution)/shard_map/dot_general | solution.py:67
  112.6 1.5 collective-permute-start.8
  114.9 2.8 collective-permute-start.9
  117.6 6.1 %copy.22 = bf16[32,24,3200]{2,1,0:T(8,128)(2,1)} copy(bf16[32,24,3200]{2,0,1:T(8,128)(2,1)} %convolution_convert_fusion.1) | data formatting | bytes 9830400 | tf_op jit(solution)/shard_map/convert_element_type | solution.py:440
  123.7 2.4 collective-permute-start.10
  126.1 2.0 collective-permute-done.10
  128.8 1.4 constant_dynamic-update-slice_fusion.13
  130.3 14.4 %collective-permute-done.6 = bf16[800,768]{1,0:T(8,128)(2,1)} collective-permute-done((bf16[800,768]{1,0:T(8,128)(2,1)S(1)}, bf16[800,768]{1,0:T(8,128)(2,1)}, u32[]{:S(2)}, u32[]{:S(2)}) %collective-permute-start.6) | collective-permute-done | bytes 1228832 | tf_op jit(solution)/shard_map/ppermute | solution.py:456
  144.6 1.4 constant_dynamic-update-slice_fusion.12
  146.2 8.4 %bitcast_add_fusion.own = bf16[768,3200]{1,0:T(8,128)(2,1)} fusion(bf16[768,3200]{1,0:T(8,128)(2,1)} %collective-permute-done.4, bf16[32,24,3200]{2,1,0:T(8,128)(2,1)} %copy.22), kind=kLoop, calls=%fused_computation.28 | loop fusion | flops 2457600 | bytes 14745600 | tf_op jit(solution)/shard_map/add | solution.py:444
  154.6 217.6 %shard_map.122 = f32[1536,768]{1,0:T(8,128)} custom-call(bf16[768,3200]{1,0:T(8,128)(2,1)} %bitcast_add_fusion.own, bf16[3200,768]{1,0:T(8,128)(2,1)} %copy-done.7, f32[1,3200]{1,0:T(1,128)S(1)} %reshape.237.gain), custom_call_target="tpu_custom_call" | custom-call | flops 7549747200 | bytes 419430400 | tf_op jit(solution)/shard_map/pallas_call | solution.py:359
  372.2 2.6 convert.5
  374.8 1.7 multiply_convert_fusion
  376.6 0.9 pad_slice_fusion.9
  377.8 0.8 pad_slice_fusion.11
  378.6 1.0 pad_slice_fusion.5
  379.6 5.2 %fusion.122 = (f32[8,192]{1,0:T(8,128)}, f32[8,192,576]{2,1,0:T(8,128)}) fusion(s32[8,576]{1,0:T(8,128)} %pad_add_fusion, s32[8,192]{1,0:T(8,128)S(1)} %broadcast_in_dim.85, bf16[8,192,128]{2,1,0:T(8,128)(2,1)S(1)} %bitcast.119, bf16[8,192,128]{2,1,0:T(8,128)(2,1)} %bitcast.125, bf16[8,192,128]{2,1,0:T(8,128)(2,1)S(1)} %bitcast.117, ...), kind=kOutput, calls=%fused_computation.184 | convolution fusion | flops 234455616 | bytes 5142528 | tf_op jit(solution)/shard_map/sub | solution.py:77
  384.8 4.6 %fusion.119 = (f32[8,192]{1,0:T(8,128)S(1)}, f32[8,192,576]{2,1,0:T(8,128)}) fusion(s32[8,576]{1,0:T(8,128)} %pad_add_fusion, s32[8,192]{1,0:T(8,128)S(1)} %broadcast_in_dim.85, bf16[8,192,128]{2,1,0:T(8,128)(2,1)S(1)} %bitcast.118, bf16[8,192,128]{2,1,0:T(8,128)(2,1)} %bitcast.127, bf16[8,192,128]{2,1,0:T(8,128)(2,1)S(1)} %bitcast.116, ...), kind=kOutput, calls=%fused_computation.183 | convolution fusion | flops 234455616 | bytes 5142528 | tf_op jit(solution)/shard_map/sub | solution.py:77
  389.4 3.1 fusion.32
  393.6 23.4 %all_to_all.10 = bf16[8,192,256]{2,1,0:T(8,128)(2,1)S(1)} all-to-all(bf16[8,192,256]{2,1,0:T(8,128)(2,1)S(1)} %pad_maximum_fusion.4), channel_id=1, replica_groups=mesh['grp'=4,'chip'=4,'core'=2] {'chip','core'}, dimensions={0} | all-to-all | bytes 1572864 | tf_op jit(solution)/shard_map/all_to_all | solution.py:500
  (111 shorter events, 17.2 us)
Async XLA Ops:
  0.6 103.9 %copy-start = (f32[256]{0:T(256)S(1)}, f32[256]{0:T(256)}, u32[]{:S(2)}) copy-start(f32[256]{0:T(256)} %param.14) | copy-start | bytes 3076
  3.9 17.9 %copy-start.14 = (s32[1,8]{1,0:T(1,128)S(1)}, s32[1,8]{1,0:T(1,128)}, u32[]{:S(2)}) copy-start(s32[1,8]{1,0:T(1,128)} %param.17) | copy-start | bytes 100
  3.9 18.0 %copy-start.15 = (s32[1,8]{1,0:T(1,128)S(1)}, s32[1,8]{1,0:T(1,128)}, u32[]{:S(2)}) copy-start(s32[1,8]{1,0:T(1,128)} %param.18) | copy-start | bytes 100
  9.9 76.1 %all-to-all-start = ((bf16[8,100,768]{2,1,0:T(8,128)(2,1)}), bf16[8,100,768]{2,1,0:T(8,128)(2,1)S(1)}, u32[]{:S(2)}, u32[]{:S(2)}) async-start(bf16[8,100,768]{2,1,0:T(8,128)(2,1)} %constant_dynamic-update-slice_fusion), calls=%async_computation | async-start | bytes 2555904 | tf_op jit(solution)/shard_map/all_to_all | solution.py:450
  17.1 23.4 %collective-permute-start = (bf16[1,128,256]{2,1,0:T(8,128)(2,1)S(1)}, bf16[1,128,256]{2,1,0:T(8,128)(2,1)S(1)}, u32[]{:S(2)}, u32[]{:S(2)}) collective-permute-start(bf16[1,128,256]{2,1,0:T(8,128)(2,1)S(1)} %get-tuple-element.19), channel_id=1, source_target_pairs={{0,8},{8,16},{16,24},{1,9},{9,17},{17,25},{2,10},{10,18},{18,26},{... | collective-permute-start | bytes 196616 | tf_op jit(solution)/shard_map/ppermute | solution.py:30
  20.5 20.1 %collective-permute-start.1 = (bf16[1,128,256]{2,1,0:T(8,128)(2,1)S(1)}, bf16[1,128,256]{2,1,0:T(8,128)(2,1)S(1)}, u32[]{:S(2)}, u32[]{:S(2)}) collective-permute-start(bf16[1,128,256]{2,1,0:T(8,128)(2,1)S(1)} %get-tuple-element.18), channel_id=1, source_target_pairs={{8,0},{16,8},{24,16},{9,1},{17,9},{25,17},{10,2},{18,10},{26,18},{... | collective-permute-start | bytes 196616 | tf_op jit(solution)/shard_map/ppermute | solution.py:30
  31.7 114.5 %collective-permute-start.4 = (bf16[768,3200]{1,0:T(8,128)(2,1)}, bf16[768,3200]{1,0:T(8,128)(2,1)}, u32[]{:S(2)}, u32[]{:S(2)}) collective-permute-start(bf16[768,3200]{1,0:T(8,128)(2,1)} %bitcast.17), channel_id=1, source_target_pairs={{0,1},{1,0},{2,3},{3,2},{4,5},{5,4},{6,7},{7,6},{8,9},{9,8},{10,11... | collective-permute-start | bytes 14745608 | tf_op jit(solution)/shard_map/ppermute | solution.py:44
  31.9 6.1 %copy-start.16 = (s32[1,32]{1,0:T(1,128)S(1)}, s32[1,32]{1,0:T(1,128)}, u32[]{:S(2)}) copy-start(s32[1,32]{1,0:T(1,128)} %param.16) | copy-start | bytes 388
  31.9 6.6 %copy-start.13 = (s32[1,64]{1,0:T(1,128)S(1)}, s32[1,64]{1,0:T(1,128)}, u32[]{:S(2)}) copy-start(s32[1,64]{1,0:T(1,128)} %param.19) | copy-start | bytes 772
  40.5 9.5 %copy-start.8 = (bf16[2304,256]{1,0:T(8,128)(2,1)S(1)}, bf16[2304,256]{1,0:T(8,128)(2,1)}, u32[]{:S(2)}) copy-start(bf16[2304,256]{1,0:T(8,128)(2,1)} %param.12) | copy-start | bytes 3538948
  46.4 9.4 %collective-permute-start.2 = (bf16[66,1,256]{2,1,0:T(2,128)(2,1)S(1)}, bf16[66,1,256]{2,1,0:T(2,128)(2,1)S(1)}, u32[]{:S(2)}, u32[]{:S(2)}) collective-permute-start(bf16[66,1,256]{2,1,0:T(2,128)(2,1)S(1)} %get-tuple-element.13), channel_id=1, source_target_pairs={{0,1},{1,2},{2,3},{3,4},{4,5},{5,6},{6,7},{8,9},{9,10},{10,11},{11... | collective-permute-start | bytes 101384 | tf_op jit(solution)/shard_map/ppermute | solution.py:30
  48.6 7.2 %collective-permute-start.3 = (bf16[66,1,256]{2,1,0:T(2,128)(2,1)S(1)}, bf16[66,1,256]{2,1,0:T(2,128)(2,1)S(1)}, u32[]{:S(2)}, u32[]{:S(2)}) collective-permute-start(bf16[66,1,256]{2,1,0:T(2,128)(2,1)S(1)} %get-tuple-element.14), channel_id=1, source_target_pairs={{1,0},{2,1},{3,2},{4,3},{5,4},{6,5},{7,6},{9,8},{10,9},{11,10},{12... | collective-permute-start | bytes 101384 | tf_op jit(solution)/shard_map/ppermute | solution.py:30
  68.2 2.2 copy-start.4
  70.4 2.2 copy-start.3
  72.6 2.2 copy-start.5
  74.8 4.5 %copy-start.1 = (bf16[64,128,256]{2,1,0:T(8,128)(2,1)S(1)}, bf16[64,128,256]{2,1,0:T(8,128)(2,1)}, u32[]{:S(2)}) copy-start(bf16[64,128,256]{2,1,0:T(8,128)(2,1)} %param.11) | copy-start | bytes 12582916
  79.3 2.2 copy-start.2
  81.5 7.7 %copy-start.12 = (f32[256]{0:T(256)S(1)}, f32[256]{0:T(256)}, u32[]{:S(2)}) copy-start(f32[256]{0:T(256)} %param.13) | copy-start | bytes 3076
  86.2 42.6 %collective-permute-start.5 = (bf16[800,768]{1,0:T(8,128)(2,1)S(1)}, bf16[800,768]{1,0:T(8,128)(2,1)}, u32[]{:S(2)}, u32[]{:S(2)}) collective-permute-start(bf16[800,768]{1,0:T(8,128)(2,1)S(1)} %reshape.236), channel_id=1, source_target_pairs={{0,8},{8,16},{16,24},{24,0},{1,9},{9,17},{17,25},{25,1},{2,10},{10... | collective-permute-start | bytes 3686408 | tf_op jit(solution)/shard_map/ppermute | solution.py:456
  100.6 44.0 %collective-permute-start.6 = (bf16[800,768]{1,0:T(8,128)(2,1)S(1)}, bf16[800,768]{1,0:T(8,128)(2,1)}, u32[]{:S(2)}, u32[]{:S(2)}) collective-permute-start(bf16[800,768]{1,0:T(8,128)(2,1)S(1)} %reshape.236), channel_id=1, source_target_pairs={{0,16},{8,24},{16,0},{24,8},{1,17},{9,25},{17,1},{25,9},{2,18},{10... | collective-permute-start | bytes 3686408 | tf_op jit(solution)/shard_map/ppermute | solution.py:456
  102.2 43.8 %collective-permute-start.7 = (bf16[800,768]{1,0:T(8,128)(2,1)S(1)}, bf16[800,768]{1,0:T(8,128)(2,1)S(1)}, u32[]{:S(2)}, u32[]{:S(2)}) collective-permute-start(bf16[800,768]{1,0:T(8,128)(2,1)S(1)} %reshape.236), channel_id=1, source_target_pairs={{0,24},{8,0},{16,8},{24,16},{1,25},{9,1},{17,9},{25,17},{2,26},{10... | collective-permute-start | bytes 3686408 | tf_op jit(solution)/shard_map/ppermute | solution.py:456
  111.6 12.0 %copy-start.6 = (f32[1,8192]{1,0:T(1,128)}, f32[1,8192]{1,0:T(1,128)S(1)}, u32[]{:S(2)}) copy-start(f32[1,8192]{1,0:T(1,128)S(1)} %fusion.125) | copy-start | bytes 98308
  112.6 2.3 collective-permute-start.8
  114.9 8.8 %collective-permute-start.9 = (f32[64]{0:T(128)S(1)}, f32[64]{0:T(128)S(1)}, u32[]{:S(2)}, u32[]{:S(2)}) collective-permute-start(f32[64]{0:T(128)S(1)} %add.171), channel_id=1, source_target_pairs={{0,2},{2,0},{4,6},{6,4},{1,3},{3,1},{5,7},{7,5},{8,10},{10,8},{12,... | collective-permute-start | bytes 776 | tf_op jit(solution)/shard_map/ppermute | solution.py:384
  117.6 8.5 %copy-start.10 = (f32[3200]{0:T(1024)S(1)}, f32[3200]{0:T(1024)}, u32[]{:S(2)}) copy-start(f32[3200]{0:T(1024)} %param.20) | copy-start | bytes 38404
  123.7 4.5 %collective-permute-start.10 = (f32[64]{0:T(128)S(1)}, f32[64]{0:T(128)S(1)}, u32[]{:S(2)}, u32[]{:S(2)}) collective-permute-start(f32[64]{0:T(128)S(1)} %add.172), channel_id=1, source_target_pairs={{0,4},{2,6},{4,0},{6,2},{1,5},{3,7},{5,1},{7,3},{8,12},{10,14},{12... | collective-permute-start | bytes 776 | tf_op jit(solution)/shard_map/ppermute | solution.py:384
  146.1 8.5 %copy-start.7 = (bf16[3200,768]{1,0:T(8,128)(2,1)}, bf16[3200,768]{1,0:T(8,128)(2,1)S(1)}, u32[]{:S(2)}) copy-start(bf16[3200,768]{1,0:T(8,128)(2,1)S(1)} %constant_dynamic-update-slice_fusion.11.weight) | copy-start | bytes 14745604
  384.8 4.6 %copy-start.9 = (bf16[1536,128]{1,0:T(8,128)(2,1)S(1)}, bf16[1536,128]{1,0:T(8,128)(2,1)}, u32[]{:S(2)}) copy-start(bf16[1536,128]{1,0:T(8,128)(2,1)} %get-tuple-element.34) | copy-start | bytes 1179652
  384.8 4.6 %copy-start.18 = (f32[8,192]{1,0:T(8,128)S(1)}, f32[8,192]{1,0:T(8,128)}, u32[]{:S(2)}) copy-start(f32[8,192]{1,0:T(8,128)} %get-tuple-element.45) | copy-start | bytes 18436
  389.4 3.3 copy-start.17
  417.1 0.8 copy-start.11
